TPU v7x, 256 devices: a whole 4x4x8 slice. The times are simulated.
256 devices in a mesh: band: 64 (over y, z, core), pos: 4 (over x).
Axes of the slice: x: 4, y: 4, z: 8, core: 2. Of those that a mesh axis runs over, the one named last changes fastest.
Arguments:
- object_field: float32 [2, 12288, 512], P(None, 'band'), may hold values from -6 to 6
- probe: float32 [2, 256, 256], replicated, may hold values from -6 to 6
- measured: bfloat16 [3072, 256, 256], P(('band', 'pos')), may hold values from 0 to 2
- row_offset: int32 [3072], P(('band', 'pos')), may hold values from 0 to 191
- col_offset: int32 [3072], P(('band', 'pos')), may hold values from 0 to 256
- counts: int32 [256], P(('band', 'pos')), may hold values from 1 to 12, 1024 in all
Outputs:
- object_grad: float32 [2, 12288, 512], P(None, 'band')
- probe_grad: float32 [2, 256, 256], replicated
Inputs may be any that keep to these rules, and one draw needn't show every extreme that they name: The counts sum to 1024; the busiest device has exactly 12 live slots.
All inputs are finite; a program needn't handle non-finite values.
Results may differ from a plain program's by a relative error of at most 0.0018.
The roundings to bfloat16 on the way count: a program that leaves them out, or rounds other values in their place, can miss the bound.
Values may be sent and summed in bfloat16 or wider, within the bound.
A program may use at most 64 MiB of HBM per device.

v0:
```python
import math

import jax
import jax.numpy as jnp
from jax import lax
from jax.sharding import PartitionSpec as P


def shifted(value, axis, steps):
    count = lax.axis_size(axis)
    initial, last = (max(0, -steps), min(count, count - steps))
    return lax.ppermute(value, axis, [(source, source + steps) for source in range(initial, last)])


def dft_tables(width):
    index = jnp.arange(width, dtype=jnp.int32)
    phase = index[:, None] * index[None, :] % width
    angle = phase.astype(jnp.float32) * (2.0 * math.pi / width)
    factor = 1.0 / math.sqrt(width)
    real_part = (jnp.cos(angle) * factor).astype(jnp.bfloat16)
    imag_part = (-jnp.sin(angle) * factor).astype(jnp.bfloat16)
    left_table = jnp.concatenate(
        [jnp.concatenate([real_part, -imag_part], 1), jnp.concatenate([imag_part, real_part], 1)], 0
    )
    right_table = jnp.concatenate(
        [jnp.concatenate([real_part, imag_part], 1), jnp.concatenate([-imag_part, real_part], 1)], 0
    )
    return (left_table, right_table)


def slot_terms(patch, probe, measured_one, live, left_table, right_table):
    width = probe.shape[1]
    patch_f = patch.astype(jnp.float32)
    exit_real = probe[0] * patch_f[0] - probe[1] * patch_f[1]
    exit_imag = probe[0] * patch_f[1] + probe[1] * patch_f[0]
    exit_wave = jnp.concatenate([exit_real, exit_imag], 0).astype(jnp.bfloat16)
    half = jnp.dot(left_table, exit_wave, preferred_element_type=jnp.float32).astype(jnp.bfloat16)
    half_row = jnp.concatenate([half[:width], half[width:]], 1)
    wave = jnp.dot(half_row, right_table, preferred_element_type=jnp.float32)
    wave_real = wave[:, :width]
    wave_imag = wave[:, width:]
    excess = (
        wave_real * wave_real + wave_imag * wave_imag - measured_one.astype(jnp.float32)
    ) * live
    resid = jnp.concatenate([wave_real * excess, wave_imag * excess], 1).astype(jnp.bfloat16)
    back = jnp.dot(resid, left_table, preferred_element_type=jnp.float32).astype(jnp.bfloat16)
    back_col = jnp.concatenate([back[:, :width], back[:, width:]], 0)
    chi = jnp.dot(right_table, back_col, preferred_element_type=jnp.float32)
    chi_real = chi[:width]
    chi_imag = chi[width:]
    grad_patch = jnp.stack(
        [probe[0] * chi_real + probe[1] * chi_imag, probe[0] * chi_imag - probe[1] * chi_real]
    )
    probe_term = jnp.stack(
        [
            patch_f[0] * chi_real + patch_f[1] * chi_imag,
            patch_f[0] * chi_imag - patch_f[1] * chi_real,
        ]
    )
    return (grad_patch, probe_term)


def on_device(object_field, probe, measured, row_offset, col_offset, counts):
    rows = object_field.shape[1]
    columns = object_field.shape[2]
    width = probe.shape[1]
    reach = (rows + width - 2) // rows
    lowered = object_field.astype(jnp.bfloat16)
    pieces = [lowered]
    for step in range(1, reach + 1):
        pieces.append(shifted(lowered, "band", -step))
    window = jnp.concatenate(pieces, 1)
    left_table, right_table = dft_tables(width)
    live_count = counts[0]
    slots = measured.shape[0]

    def visit(carry, item):
        grad_window, probe_sum = carry
        measured_one, top, start, index = item
        zero = jnp.int32(0)
        patch = lax.dynamic_slice(window, (zero, top, start), (2, width, width))
        live = (index < live_count).astype(jnp.float32)
        grad_patch, probe_term = slot_terms(
            patch, probe, measured_one, live, left_table, right_table
        )
        current = lax.dynamic_slice(grad_window, (zero, top, start), (2, width, width))
        grad_window = lax.dynamic_update_slice(
            grad_window, current + grad_patch, (zero, top, start)
        )
        return ((grad_window, probe_sum + probe_term), None)

    initial = (
        jnp.zeros((2, (reach + 1) * rows, columns), jnp.float32),
        jnp.zeros((2, width, width), jnp.float32),
    )
    (grad_window, probe_sum), _ = lax.scan(
        visit, initial, (measured, row_offset, col_offset, jnp.arange(slots, dtype=jnp.int32))
    )
    summed = lax.psum(grad_window, "pos")
    object_grad = summed[:, :rows]
    for step in range(1, reach + 1):
        object_grad = object_grad + shifted(
            summed[:, step * rows : (step + 1) * rows], "band", step
        )
    total = lax.psum(probe_sum, ("band", "pos"))
    shards = lax.axis_size("band") * lax.axis_size("pos")
    mean_slots = slots // 3
    probe_grad = total * (1.0 / math.sqrt(shards * mean_slots))
    return (object_grad, probe_grad)


def solution(mesh):
    placed = (
        P(None, "band", None),
        P(),
        P(("band", "pos"), None, None),
        P(("band", "pos")),
        P(("band", "pos")),
        P(("band", "pos")),
    )
    return jax.shard_map(
        on_device,
        mesh=mesh,
        in_specs=placed,
        out_specs=(P(None, "band", None), P()),
        check_vma=False,
    )
```

profile of v0, /device:TPU:1, one launch (start us, length us, event | category | flops | bytes accessed | tf_op | source)
XLA Modules:
  0.0 653.4 jit_solution(5862271410070495877)
XLA Ops:
  10.7 5.1 collective-permute-start
  20.1 3.4 collective-permute-done.1
  23.5 8.1 %collective-permute-done = bf16[2,192,512]{1,2,0:T(8,128)(2,1)S(1)} collective-permute-done((bf16[2,192,512]{1,2,0:T(8,128)(2,1)S(1)}, bf16[2,192,512]{1,2,0:T(8,128)(2,1)S(1)}, u32[]{:S(2)}, u32[]{:S(2)}) %collective-permute-start) | collective-permute-done | bytes 393248 | tf_op jit(solution)/shard_map/ppermute | solution.py:12
  31.6 1.6 pad_maximum_fusion
  33.1 1.7 broadcast_in_dim.8.clone
  34.8 277.6 %while.13 = (s32[]{:T(128)}, f32[2,576,512]{2,1,0:T(8,128)}, f32[2,256,256]{1,2,0:T(8,128)}, s32[12]{0:T(128)S(1)}, s32[12]{0:T(128)S(1)}, /*index=5*/f32[2,256,...) while((s32[]{:T(128)}, f32[2,576,512]{2,1,0:T(8,128)}, ...), condition=%wide.region_1.2_spmd.clone, body=%wide.region_0.1_spmd.clone.sunk | while | flops 541982720 | bytes 18743608 | solution.py:96
  43.1 1.4 fusion.66
  45.8 1.3 convolution_convert_fusion.3
  47.6 1.4 constant_dynamic-slice_fusion.2
  50.4 6.5 dynamic_update_slice.5
  65.1 1.4 fusion.66
  67.8 1.3 convolution_convert_fusion.3
  69.6 1.4 constant_dynamic-slice_fusion.2
  71.2 2.0 maximum_add_fusion.3
  73.4 6.8 %dynamic_update_slice.5 = f32[2,576,512]{2,1,0:T(8,128)} dynamic-update-slice(f32[2,576,512]{2,1,0:T(8,128)} %get-tuple-element.282, f32[2,256,256]{2,1,0:T(8,128)S(1)} %copy.18, s32[]{:T(128)} %constant.17.clone.1..sunk, s32[]{:T(128)S(6)} %select_n.47, s32[]{:T(128)S(6)} %select_n.48) | dynamic-update-slice | bytes 1048580 | tf_op jit(solution)/shard_map/while/body/eval_jaxpr/dynamic_update_slice | solution.py:87
  88.4 1.4 fusion.66
  91.1 1.3 convolution_convert_fusion.3
  93.0 1.4 constant_dynamic-slice_fusion.2
  94.6 2.0 maximum_add_fusion.3
  96.7 6.7 %dynamic_update_slice.5 = f32[2,576,512]{2,1,0:T(8,128)} dynamic-update-slice(f32[2,576,512]{2,1,0:T(8,128)} %get-tuple-element.282, f32[2,256,256]{2,1,0:T(8,128)S(1)} %copy.18, s32[]{:T(128)} %constant.17.clone.1..sunk, s32[]{:T(128)S(6)} %select_n.47, s32[]{:T(128)S(6)} %select_n.48) | dynamic-update-slice | bytes 1048580 | tf_op jit(solution)/shard_map/while/body/eval_jaxpr/dynamic_update_slice | solution.py:87
  111.6 1.4 fusion.66
  114.4 1.3 convolution_convert_fusion.3
  116.2 1.4 constant_dynamic-slice_fusion.2
  117.8 2.0 maximum_add_fusion.3
  120.0 6.6 %dynamic_update_slice.5 = f32[2,576,512]{2,1,0:T(8,128)} dynamic-update-slice(f32[2,576,512]{2,1,0:T(8,128)} %get-tuple-element.282, f32[2,256,256]{2,1,0:T(8,128)S(1)} %copy.18, s32[]{:T(128)} %constant.17.clone.1..sunk, s32[]{:T(128)S(6)} %select_n.47, s32[]{:T(128)S(6)} %select_n.48) | dynamic-update-slice | bytes 1048580 | tf_op jit(solution)/shard_map/while/body/eval_jaxpr/dynamic_update_slice | solution.py:87
  134.8 1.4 fusion.66
  139.4 1.4 constant_dynamic-slice_fusion.2
  140.9 2.0 maximum_add_fusion.3
  143.1 6.7 %dynamic_update_slice.5 = f32[2,576,512]{2,1,0:T(8,128)} dynamic-update-slice(f32[2,576,512]{2,1,0:T(8,128)} %get-tuple-element.282, f32[2,256,256]{2,1,0:T(8,128)S(1)} %copy.18, s32[]{:T(128)} %constant.17.clone.1..sunk, s32[]{:T(128)S(6)} %select_n.47, s32[]{:T(128)S(6)} %select_n.48) | dynamic-update-slice | bytes 1048580 | tf_op jit(solution)/shard_map/while/body/eval_jaxpr/dynamic_update_slice | solution.py:87
  158.0 1.4 fusion.66
  162.6 1.4 constant_dynamic-slice_fusion.2
  164.2 2.0 maximum_add_fusion.3
  166.4 6.5 dynamic_update_slice.5
  181.1 1.4 fusion.66
  185.7 1.4 constant_dynamic-slice_fusion.2
  187.3 2.0 maximum_add_fusion.3
  189.5 6.7 %dynamic_update_slice.5 = f32[2,576,512]{2,1,0:T(8,128)} dynamic-update-slice(f32[2,576,512]{2,1,0:T(8,128)} %get-tuple-element.282, f32[2,256,256]{2,1,0:T(8,128)S(1)} %copy.18, s32[]{:T(128)} %constant.17.clone.1..sunk, s32[]{:T(128)S(6)} %select_n.47, s32[]{:T(128)S(6)} %select_n.48) | dynamic-update-slice | bytes 1048580 | tf_op jit(solution)/shard_map/while/body/eval_jaxpr/dynamic_update_slice | solution.py:87
  204.4 1.4 fusion.66
  208.9 1.4 constant_dynamic-slice_fusion.2
  210.5 2.0 maximum_add_fusion.3
  212.7 6.5 dynamic_update_slice.5
  227.4 1.4 fusion.66
  232.0 1.4 constant_dynamic-slice_fusion.2
  233.6 2.0 maximum_add_fusion.3
  235.8 6.8 %dynamic_update_slice.5 = f32[2,576,512]{2,1,0:T(8,128)} dynamic-update-slice(f32[2,576,512]{2,1,0:T(8,128)} %get-tuple-element.282, f32[2,256,256]{2,1,0:T(8,128)S(1)} %copy.18, s32[]{:T(128)} %constant.17.clone.1..sunk, s32[]{:T(128)S(6)} %select_n.47, s32[]{:T(128)S(6)} %select_n.48) | dynamic-update-slice | bytes 1048580 | tf_op jit(solution)/shard_map/while/body/eval_jaxpr/dynamic_update_slice | solution.py:87
  250.8 1.4 fusion.66
  255.4 1.4 constant_dynamic-slice_fusion.2
  257.0 2.0 maximum_add_fusion.3
  259.2 6.6 %dynamic_update_slice.5 = f32[2,576,512]{2,1,0:T(8,128)} dynamic-update-slice(f32[2,576,512]{2,1,0:T(8,128)} %get-tuple-element.282, f32[2,256,256]{2,1,0:T(8,128)S(1)} %copy.18, s32[]{:T(128)} %constant.17.clone.1..sunk, s32[]{:T(128)S(6)} %select_n.47, s32[]{:T(128)S(6)} %select_n.48) | dynamic-update-slice | bytes 1048580 | tf_op jit(solution)/shard_map/while/body/eval_jaxpr/dynamic_update_slice | solution.py:87
  274.0 1.4 fusion.66
  278.6 1.4 constant_dynamic-slice_fusion.2
  280.1 2.0 maximum_add_fusion.3
  282.3 6.8 %dynamic_update_slice.5 = f32[2,576,512]{2,1,0:T(8,128)} dynamic-update-slice(f32[2,576,512]{2,1,0:T(8,128)} %get-tuple-element.282, f32[2,256,256]{2,1,0:T(8,128)S(1)} %copy.18, s32[]{:T(128)} %constant.17.clone.1..sunk, s32[]{:T(128)S(6)} %select_n.47, s32[]{:T(128)S(6)} %select_n.48) | dynamic-update-slice | bytes 1048580 | tf_op jit(solution)/shard_map/while/body/eval_jaxpr/dynamic_update_slice | solution.py:87
  297.3 1.4 fusion.66
  301.9 1.4 constant_dynamic-slice_fusion.2
  303.5 2.0 maximum_add_fusion.3
  305.7 6.8 %dynamic_update_slice.5 = f32[2,576,512]{2,1,0:T(8,128)} dynamic-update-slice(f32[2,576,512]{2,1,0:T(8,128)} %get-tuple-element.282, f32[2,256,256]{2,1,0:T(8,128)S(1)} %copy.18, s32[]{:T(128)} %constant.17.clone.1..sunk, s32[]{:T(128)S(6)} %select_n.47, s32[]{:T(128)S(6)} %select_n.48) | dynamic-update-slice | bytes 1048580 | tf_op jit(solution)/shard_map/while/body/eval_jaxpr/dynamic_update_slice | solution.py:87
  312.6 70.6 %all-reduce.3.cloned.1.call-done = f32[2,576,512]{2,1,0:T(8,128)} async-done(((f32[2,576,512]{2,1,0:T(8,128)}), f32[2,576,512]{2,1,0:T(8,128)}) %all-reduce.3.cloned.1.call-update) | async-done | bytes 2359312 | tf_op jit(solution)/shard_map/psum | solution.py:99
  383.2 2.4 fusion.39
  385.6 3.7 collective-permute-start.2
  389.3 3.2 collective-permute-start.3
  393.6 248.2 %all-reduce.5.cloned.1.call-done = f32[2,256,256]{2,1,0:T(8,128)} async-done(((f32[2,256,256]{2,1,0:T(8,128)}), f32[2,256,256]{2,1,0:T(8,128)}) %all-reduce.5.cloned.1.call-update) | async-done | bytes 524304 | tf_op jit(solution)/shard_map/psum | solution.py:105
  641.8 1.9 broadcast_multiply_fusion
  643.7 2.3 fusion.27
  (186 shorter events, 83.4 us)
Async XLA Ops:
  8.0 375.2 %all-reduce.3.cloned.1.call-start = ((), (), s32[]{:S(2)}) async-start(), calls=%async_computation | async-start | bytes 4718592 | tf_op jit(solution)/shard_map/psum | solution.py:99
  9.4 14.1 %collective-permute-start.1 = (bf16[2,192,512]{1,2,0:T(8,128)(2,1)S(1)}, bf16[2,192,512]{1,2,0:T(8,128)(2,1)S(1)}, u32[]{:S(2)}, u32[]{:S(2)}) collective-permute-start(bf16[2,192,512]{1,2,0:T(8,128)(2,1)S(1)} %copy.8), channel_id=1, source_target_pairs={{8,0},{12,4},{16,8},{20,12},{24,16},{28,20},{32,24},{36,28},{40,32... | collective-permute-start | bytes 1179656 | tf_op jit(solution)/shard_map/ppermute | solution.py:12
  10.7 20.9 %collective-permute-start = (bf16[2,192,512]{1,2,0:T(8,128)(2,1)S(1)}, bf16[2,192,512]{1,2,0:T(8,128)(2,1)S(1)}, u32[]{:S(2)}, u32[]{:S(2)}) collective-permute-start(bf16[2,192,512]{1,2,0:T(8,128)(2,1)S(1)} %copy.8), channel_id=1, source_target_pairs={{4,0},{8,4},{12,8},{16,12},{20,16},{24,20},{28,24},{32,28},{36,32}... | collective-permute-start | bytes 1179656 | tf_op jit(solution)/shard_map/ppermute | solution.py:12
  20.1 14.8 %copy-start.1 = (s32[12]{0:T(128)S(1)}, s32[12]{0:T(128)}, u32[]{:S(2)}) copy-start(s32[12]{0:T(128)} %param.11) | copy-start | bytes 148
  20.1 14.8 %copy-start.2 = (s32[12]{0:T(128)S(1)}, s32[12]{0:T(128)}, u32[]{:S(2)}) copy-start(s32[12]{0:T(128)} %param.12) | copy-start | bytes 148
  312.5 80.1 %copy-start = (f32[2,256,256]{1,2,0:T(8,128)S(1)}, f32[2,256,256]{1,2,0:T(8,128)}, u32[]{:S(2)}) copy-start(f32[2,256,256]{1,2,0:T(8,128)} %get-tuple-element.66) | copy-start | bytes 1572868
  312.5 329.3 %all-reduce.5.cloned.1.call-start = ((), (), s32[]{:S(2)}) async-start(), calls=%async_computation.1 | async-start | bytes 1048576 | tf_op jit(solution)/shard_map/psum | solution.py:105
  385.6 258.1 %collective-permute-start.2 = (f32[2,192,512]{2,1,0:T(8,128)}, f32[2,192,512]{2,1,0:T(8,128)S(1)}, u32[]{:S(2)}, u32[]{:S(2)}) collective-permute-start(f32[2,192,512]{2,1,0:T(8,128)} %get-tuple-element.158), channel_id=1, source_target_pairs={{0,4},{4,8},{8,12},{12,16},{16,20},{20,24},{24,28},{28,32},{32,36}... | collective-permute-start | bytes 2359304 | tf_op jit(solution)/shard_map/ppermute | solution.py:12
  389.3 254.4 %collective-permute-start.3 = (f32[2,192,512]{2,1,0:T(8,128)S(1)}, f32[2,192,512]{2,1,0:T(8,128)S(1)}, u32[]{:S(2)}, u32[]{:S(2)}) collective-permute-start(f32[2,192,512]{2,1,0:T(8,128)S(1)} %get-tuple-element.159), channel_id=1, source_target_pairs={{0,8},{4,12},{8,16},{12,20},{16,24},{20,28},{24,32},{28,36},{32,40... | collective-permute-start | bytes 2359304 | tf_op jit(solution)/shard_map/ppermute | solution.py:12
Sparse Core Ops, SparseCore 0:
  312.6 70.4 all-reduce.2
Sparse Core Ops, SparseCore 1:
  393.7 248.1 all-reduce.4
where the time goes:
time: 660 us; the launch traced here: 653 us
  waiting for transfers between devices  330 us (50%)
  local copies, waits for them, and re-layouts  131 us (20%)
  loops' own time  62.4 us (9%)
  other arithmetic  60.2 us (9%)
  matrix products  40.4 us (6%)
  between operations  15.6 us (2%)
  starting transfers between devices  13.5 us (2%)
    psum x1, waiting for transfers between devices, on_device(): total = lax.psum(probe_sum, ('band', 'pos'))  248 us
    dynamic_update_slice x24, local copies, waits for them, and re-layouts, visit(): lax.dynamic_update_slice(grad_window, current + grad_patch, (zero, top, s...  82.1 us
    psum x1, waiting for transfers between devices, on_device(): summed = lax.psum(grad_window, 'pos')  70.6 us
    another operation x1, loops' own time, on_device(): lax.scan(visit, initial, (measured, row_offset, col_offset, jnp.arange(sl...  62.4 us
    add x12, other arithmetic, visit(): current + grad_patch  22.7 us
    dynamic_slice x36, local copies, waits for them, and re-layouts, on_device(): lax.scan(visit, initial, (measured, row_offset, col_offset, jnp.arange(sl...  21.9 us
    dynamic_slice x24, local copies, waits for them, and re-layouts, visit(): lax.dynamic_slice(grad_window, (zero, top, start), (2, width, width))  18.8 us
    dot_general x12, matrix products, slot_terms(): jnp.dot(left_table, exit_wave, preferred_element_type=jnp.float32)  16.5 us
  transfers between devices with their start and end apart: 6, of which 4 were waited for; matrix products, arithmetic and copies ran while one was open for 1% of the time, Pallas kernels for 0%

commit v1 on v0

v1 whole, which is shorter than its diff:
```python
import math

import jax
import jax.numpy as jnp
import ml_dtypes
import numpy as np
from jax import lax
from jax.experimental import pallas as pl
from jax.experimental.pallas import tpu as pltpu
from jax.sharding import PartitionSpec as P

W = 256
BR = 192
NCOLS = 512
CAP = 12
LIVE = 1024
LANES = 128
BLOCKS = NCOLS // LANES
TAIL = 64
ROWS = 2 * BR + TAIL
CHIP = ROWS + BR
HALF = CHIP // 2
NX, NY, NZ = 4, 4, 8
CHIPS = NY * NZ
BANDS = 2 * CHIPS
F32 = jnp.float32
BF16 = jnp.bfloat16
MESH = pl.DeviceIdType.MESH


def tables():
    index = np.arange(W, dtype=np.int32)
    phase = index[:, None] * index[None, :] % W
    angle = phase.astype(np.float32) * np.float32(2.0 * math.pi / W)
    factor = np.float32(1.0 / math.sqrt(W))
    real = (np.cos(angle) * factor).astype(ml_dtypes.bfloat16)
    imag = (-np.sin(angle) * factor).astype(ml_dtypes.bfloat16)
    left = np.block([[real, -imag], [imag, real]])
    right = np.block([[real, imag], [-imag, real]])
    return left, right


def dot(a, b):
    return jnp.dot(a, b, preferred_element_type=F32)


def remote(src, dst, send, recv, device):
    return pltpu.make_async_remote_copy(
        src_ref=src, dst_ref=dst, send_sem=send, recv_sem=recv, device_id=device, device_id_type=MESH
    )


def signal(barrier, device):
    pl.semaphore_signal(barrier, inc=1, device_id=device, device_id_type=MESH)


def halo_kernel(obj, win, low, near, far, send, recv):
    b = lax.axis_index("band")
    barrier = pltpu.get_barrier_semaphore()
    for step in (1, 2):

        @pl.when(b + step < BANDS)
        def _():
            signal(barrier, {"band": b + step})

    low[...] = obj[...].astype(BF16)

    def copies(step):
        src, dst = (low, near) if step == 1 else (low.at[:, :TAIL], far)
        return [
            remote(src.at[plane], dst.at[plane], send.at[step - 1, plane], recv.at[step - 1, plane], {"band": b - step})
            for plane in range(2)
        ]


    @pl.when(b > 0)
    def _():
        pl.semaphore_wait(barrier, jnp.minimum(b, 2))

    for step in (1, 2):

        @pl.when(b >= step)
        def _():
            for copy in copies(step):
                copy.start()

    def fill(src, top, count):
        for plane in range(2):
            for block in range(BLOCKS):
                win[plane, block, top : top + count] = src[plane, :, block * LANES : (block + 1) * LANES].astype(F32)

    fill(low, 0, BR)
    for step, src, top, count in ((1, near, BR, BR), (2, far, 2 * BR, TAIL)):

        @pl.when(b + step < BANDS)
        def _():
            for copy in copies(step):
                copy.wait_recv()
            fill(src, top, count)

        @pl.when(b + step >= BANDS)
        def _():
            win[:, :, top : top + count] = jnp.zeros((2, BLOCKS, count, LANES), F32)

    for step in (1, 2):

        @pl.when(b >= step)
        def _():
            for copy in copies(step):
                copy.wait_send()


def slots_kernel(cnt, row, col, win, probe, meas, left, right, grad, psum, mbuf, sems):
    n = cnt[0]

    def fetch(s):
        return pltpu.make_async_copy(meas.at[s], mbuf.at[s], sems.at[s])

    def start(s, carry):
        fetch(s).start()
        return carry

    lax.fori_loop(0, n, start, 0)
    grad[...] = jnp.zeros_like(grad)
    psum[...] = jnp.zeros_like(psum)
    lane = lax.broadcasted_iota(jnp.int32, (W, LANES), 1)

    def body(s, carry):
        r = row[s]
        c = col[s]
        block = jnp.where(c >= LANES, 1, 0)
        shift = c - LANES * block
        back = lax.rem(LANES - shift, LANES)
        ahead = lax.rem(shift, LANES)
        head = lane < LANES - shift

        def patch(plane):
            parts = [pltpu.roll(win[plane, block + j, pl.ds(r, W), :], back, 1) for j in range(3)]
            return jnp.concatenate([jnp.where(head, parts[0], parts[1]), jnp.where(head, parts[1], parts[2])], 1)

        pr, pi = patch(0), patch(1)
        qr, qi = probe[0], probe[1]
        exit_wave = jnp.concatenate([qr * pr - qi * pi, qr * pi + qi * pr], 0).astype(BF16)
        half = dot(left[...], exit_wave).astype(BF16)
        wave = dot(jnp.concatenate([half[:W], half[W:]], 1), right[...])
        wr, wi = wave[:, :W], wave[:, W:]
        fetch(s).wait()
        excess = wr * wr + wi * wi - mbuf[s].astype(F32)
        resid = jnp.concatenate([wr * excess, wi * excess], 1).astype(BF16)
        back_wave = dot(resid, left[...]).astype(BF16)
        chi = dot(right[...], jnp.concatenate([back_wave[:, :W], back_wave[:, W:]], 0))
        cr, ci = chi[:W], chi[W:]
        psum[0] += pr * cr + pi * ci
        psum[1] += pr * ci - pi * cr
        tail = lane >= shift
        for plane, g in enumerate((qr * cr + qi * ci, qr * ci - qi * cr)):
            g0 = pltpu.roll(g[:, :LANES], ahead, 1)
            g1 = pltpu.roll(g[:, LANES:], ahead, 1)
            grad[plane, block, pl.ds(r, W), :] += jnp.where(tail, g0, 0.0)
            grad[plane, block + 1, pl.ds(r, W), :] += jnp.where(tail, g1, g0)
            grad[plane, block + 2, pl.ds(r, W), :] += jnp.where(tail, 0.0, g1)
        return carry

    lax.fori_loop(0, n, body, 0)


def merge_kernel(
    grad, psum, out, pout,
    from_core, merged, relay_l, relay_r, from_l, from_r, from_z, final,
    pcore, psumc, py, pz, px,
    core_s, core_r, ring_s, ring_r, shift_s, shift_r, out_s, out_r, loc, pc_s, pc_r, y_s, y_r, z_s, z_r, x_s, x_r,
):
    b = lax.axis_index("band")
    p = lax.axis_index("pos")
    core = lax.rem(b, 2)
    chip = b // 2
    z = lax.rem(chip, NZ)
    y = chip // NZ
    sib = {"band": b + 1 - 2 * core}
    rp = lax.rem(p + 1, NX)
    lp = lax.rem(p + NX - 1, NX)
    op = lax.rem(p + 2, NX)
    left, right = {"pos": lp}, {"pos": rp}
    ydev = [None] + [{"band": b + 2 * NZ * (lax.rem(y + d, NY) - y)} for d in range(1, NY)]
    zdev = [None] + [{"band": b + 2 * (lax.rem(z + d, NZ) - z)} for d in range(1, NZ)]
    xdev = [None] + [{"pos": lax.rem(p + d, NX)} for d in range(1, NX)]
    sb = b + 1 - 2 * core

    barrier = pltpu.get_barrier_semaphore()
    for device in [sib, {"band": sb, "pos": lp}, {"band": sb, "pos": rp}] + xdev[1:] + ydev[1:] + zdev[1:]:
        signal(barrier, device)

    @pl.when(chip > 0)
    def _():
        signal(barrier, {"band": b - 2})

    @pl.when(chip < CHIPS - 1)
    def _():
        signal(barrier, {"band": b + 2})

    edges = jnp.where(chip > 0, 1, 0) + jnp.where(chip < CHIPS - 1, 1, 0)
    pl.semaphore_wait(barrier, 3 + NX - 1 + NY - 1 + NZ - 1 + edges)

    order = [op, rp, lp, p]
    to_core = [
        remote(grad.at[j // 2, 2 * (1 - core) + lax.rem(j, 2)], from_core.at[j], core_s.at[i], core_r.at[i], sib)
        for i, j in enumerate(order)
    ]
    pcopy = remote(psum.at[1 - core], pcore, pc_s.at[0], pc_r.at[0], sib)
    for copy in to_core:
        copy.start()
    pcopy.start()

    def merge(i):
        j = order[i]
        to_core[i].wait_recv()
        merged[j, pl.ds(ROWS * (1 - core), BR), :] = jnp.zeros((BR, LANES), F32)
        merged[j, pl.ds(BR * core, ROWS), :] = grad[j // 2, 2 * core + lax.rem(j, 2)]
        merged[j, pl.ds(BR * (1 - core), ROWS), :] += from_core[j]

    top, low = pl.ds(0, HALF), pl.ds(HALF, HALF)
    a_r = remote(merged.at[op, top], relay_l, ring_s.at[0], ring_r.at[0], right)
    a_l = remote(merged.at[op, low], relay_r, ring_s.at[1], ring_r.at[1], left)
    b_r = remote(merged.at[rp, low], from_l.at[low], ring_s.at[2], ring_r.at[2], right)
    b_l = remote(merged.at[lp, top], from_r.at[top], ring_s.at[3], ring_r.at[3], left)
    c_r = remote(merged.at[rp, top], from_l.at[top], ring_s.at[4], ring_r.at[4], right)
    c_l = remote(merged.at[lp, low], from_r.at[low], ring_s.at[5], ring_r.at[5], left)
    merge(0)
    a_r.start()
    a_l.start()
    merge(1)
    b_r.start()
    merge(2)
    b_l.start()

    pcopy.wait_recv()
    psumc[...] = psum[core] + pcore[...]
    yc = [None]
    for d in range(1, NY):
        yd = lax.rem(y + d, NY)
        yc.append(remote(psumc.at[pl.ds(64 * yd, 64)], py.at[d], y_s.at[d], y_r.at[d], ydev[d]))
        yc[d].start()

    a_r.wait_recv()
    merged[rp, top, :] += relay_l[...]
    c_r.start()
    a_l.wait_recv()
    merged[lp, low, :] += relay_r[...]
    c_l.start()
    merge(3)

    for d in range(1, NY):
        yc[d].wait_recv()
    py[0] = psumc[pl.ds(64 * y, 64), :] + py[1] + py[2] + py[3]
    zc = [None]
    for d in range(1, NZ):
        zd = lax.rem(z + d, NZ)
        zc.append(remote(py.at[0, pl.ds(8 * zd, 8)], pz.at[d], z_s.at[d], z_r.at[d], zdev[d]))
        zc[d].start()

    b_r.wait_recv()
    b_l.wait_recv()

    for d in range(1, NZ):
        zc[d].wait_recv()
    px[p] = ((py[0, pl.ds(8 * z, 8), :] + pz[1]) + (pz[2] + pz[3])) + ((pz[4] + pz[5]) + (pz[6] + pz[7]))
    xc = [None]
    for d in range(1, NX):
        xc.append(remote(px.at[p], px.at[p], x_s.at[d], x_r.at[d], xdev[d]))
        xc[d].start()

    c_l.wait_recv()
    c_r.wait_recv()
    own, below = pl.ds(0, 2 * BR), pl.ds(2 * BR, CHIP - 2 * BR)
    final[below, :] = merged[p, below, :] + (from_l[below, :] + from_r[below, :])
    shift = remote(final.at[below], from_z, shift_s.at[0], shift_r.at[0], {"band": b + 2})

    @pl.when(chip < CHIPS - 1)
    def _():
        shift.start()

    final[own, :] = merged[p, own, :] + (from_l[own, :] + from_r[own, :])

    for d in range(1, NX):
        xc[d].wait_recv()
    zrows = pl.ds(8 * z, 8)
    prow = pl.ds(64 * y + 8 * z, 8)
    total = ((px[0] + px[1]) + (px[2] + px[3])) * F32(1.0 / math.sqrt(LIVE))
    pout[core, prow, :] = total
    zg = [None]
    for d in range(1, NZ):
        zg.append(remote(pout.at[core, prow], pout.at[core, prow], z_s.at[NZ + d], z_r.at[NZ + d], zdev[d]))
        zg[d].start()

    @pl.when(chip > 0)
    def _():
        shift.wait_recv()
        final[pl.ds(0, CHIP - 2 * BR), :] += from_z[...]

    plane = p // 2
    cols = pl.ds(pl.multiple_of(LANES * (2 * core + lax.rem(p, 2)), LANES), LANES)
    gather = []
    for c in range(2):
        src = final.at[pl.ds(BR * c, BR)]
        dst = out.at[plane, :, cols]
        for i, pos in enumerate((rp, lp)):
            k = 2 * i + c
            gather.append(remote(src, dst, out_s.at[k], out_r.at[2 * i + core], {"band": 2 * chip + c, "pos": pos}))
    for copy in gather:
        copy.start()
    sibcopy = remote(final.at[pl.ds(BR * (1 - core), BR)], out.at[plane, :, cols], out_s.at[4], out_r.at[4], sib)
    sibcopy.start()
    mine = pltpu.make_async_copy(final.at[pl.ds(BR * core, BR)], out.at[plane, :, cols], loc)
    mine.start()

    for d in range(1, NZ):
        zg[d].wait_recv()
    yrows = pl.ds(64 * y, 64)
    yg = [None]
    for d in range(1, NY):
        yg.append(remote(pout.at[core, yrows], pout.at[core, yrows], y_s.at[NY + d], y_r.at[NY + d], ydev[d]))
        yg[d].start()

    def got(i, c, pos):
        blk = pl.ds(pl.multiple_of(LANES * (2 * c + lax.rem(pos, 2)), LANES), LANES)
        return out.at[pos // 2, :, blk], out_r.at[2 * i + c]

    ref_l0, sem_l0 = got(0, 0, lp)
    ref_l1, sem_l1 = got(0, 1, lp)
    ref_r0, sem_r0 = got(1, 0, rp)
    ref_r1, sem_r1 = got(1, 1, rp)
    on_r = remote(ref_l0, ref_l0, out_s.at[5], out_r.at[5], right)
    on_l = remote(ref_r1, ref_r1, out_s.at[6], out_r.at[6], left)
    remote(ref_l0, ref_l0, out_s.at[0], sem_l0, right).wait_recv()
    on_r.start()
    remote(ref_r1, ref_r1, out_s.at[0], sem_r1, right).wait_recv()
    on_l.start()

    for d in range(1, NY):
        yg[d].wait_recv()
    plast = remote(pout.at[core], pout.at[core], pc_s.at[1], pc_r.at[1], sib)
    plast.start()

    remote(ref_l1, ref_l1, out_s.at[0], sem_l1, right).wait_recv()
    remote(ref_r0, ref_r0, out_s.at[0], sem_r0, right).wait_recv()
    sibcopy.wait_recv()
    on_r.wait_recv()
    on_l.wait_recv()
    plast.wait_recv()
    mine.wait()

    for copy in to_core + [pcopy, a_r, a_l, b_r, b_l, c_r, c_l] + yc[1:] + zc[1:] + xc[1:] + zg[1:] + yg[1:]:
        copy.wait_send()
    for copy in gather + [sibcopy, on_r, on_l, plast]:
        copy.wait_send()

    @pl.when(chip < CHIPS - 1)
    def _():
        shift.wait_send()


VM = pl.BlockSpec(memory_space=pltpu.VMEM)
SM = pl.BlockSpec(memory_space=pltpu.SMEM)
ANY = pl.BlockSpec(memory_space=pl.ANY)
DMA = pltpu.SemaphoreType.DMA


def params(cid=None):
    return pltpu.CompilerParams(vmem_limit_bytes=40 << 20, collective_id=cid, has_side_effects=cid is not None)


def halo(obj):
    return pl.pallas_call(
        halo_kernel,
        out_shape=jax.ShapeDtypeStruct((2, BLOCKS, ROWS, LANES), F32),
        in_specs=[VM],
        out_specs=VM,
        scratch_shapes=[
            pltpu.VMEM((2, BR, NCOLS), BF16),
            pltpu.VMEM((2, BR, NCOLS), BF16),
            pltpu.VMEM((2, TAIL, NCOLS), BF16),
            DMA((2, 2)),
            DMA((2, 2)),
        ],
        compiler_params=params(0),
        name="halo",
    )(obj)


def slots(counts, rows, cols, win, probe, measured, left, right):
    return pl.pallas_call(
        slots_kernel,
        out_shape=(
            jax.ShapeDtypeStruct((2, BLOCKS, ROWS, LANES), F32),
            jax.ShapeDtypeStruct((2, W, W), F32),
        ),
        in_specs=[SM, SM, SM, VM, VM, ANY, VM, VM],
        out_specs=(VM, VM),
        scratch_shapes=[pltpu.VMEM((CAP, W, W), BF16), DMA((CAP,))],
        compiler_params=params(),
        name="slots",
    )(counts, rows, cols, win, probe, measured, left, right)


def merge(grad, psum):
    piece = lambda n, *lead: pltpu.VMEM((*lead, n, LANES), F32)
    flat = lambda n, *lead: pltpu.VMEM((*lead, n, W), F32)
    return pl.pallas_call(
        merge_kernel,
        out_shape=(
            jax.ShapeDtypeStruct((2, BR, NCOLS), F32),
            jax.ShapeDtypeStruct((2, W, W), F32),
        ),
        in_specs=[VM, VM],
        out_specs=(VM, VM),
        scratch_shapes=[
            piece(ROWS, 4),
            piece(CHIP, 4),
            piece(HALF),
            piece(HALF),
            piece(CHIP),
            piece(CHIP),
            piece(CHIP - 2 * BR),
            piece(CHIP),
            flat(W),
            flat(W),
            flat(64, NY),
            flat(8, NZ),
            flat(8, NX),
            DMA((4,)), DMA((4,)),
            DMA((6,)), DMA((6,)),
            DMA((1,)), DMA((1,)),
            DMA((7,)), DMA((7,)),
            DMA,
            DMA((2,)), DMA((2,)),
            DMA((2 * NY,)), DMA((2 * NY,)),
            DMA((2 * NZ,)), DMA((2 * NZ,)),
            DMA((NX,)), DMA((NX,)),
        ],
        compiler_params=params(1),
        name="merge",
    )(grad, psum)


def on_device(object_field, probe, measured, row_offset, col_offset, counts):
    left, right = tables()
    win = halo(object_field)
    grad, psum = slots(counts, row_offset, col_offset, win, probe, measured, left, right)
    return merge(grad, psum)


def solution(mesh):
    placed = (
        P(None, "band", None),
        P(),
        P(("band", "pos"), None, None),
        P(("band", "pos")),
        P(("band", "pos")),
        P(("band", "pos")),
    )
    return jax.shard_map(
        on_device,
        mesh=mesh,
        in_specs=placed,
        out_specs=(P(None, "band", None), P()),
        check_vma=False,
    )
```

time: 660 us -> 79.2 us (0.12)
  the two profiles are of different devices: /device:TPU:1 before, /device:TPU:11 now
where the time goes in v1:
time: 79.2 us; the launch traced here: 79 us
  Pallas kernels  73.7 us (93%)
  local copies, waits for them, and re-layouts  3.86 us (5%)
  between operations  1.49 us (2%)
    pallas_call x1, Pallas kernels, merge(): pl.pallas_call(merge_kernel, out_shape=(jax.ShapeDtypeStruct((2, BR, NCOL...  48 us
    pallas_call x1, Pallas kernels, slots(): pl.pallas_call(slots_kernel, out_shape=(jax.ShapeDtypeStruct((2, BLOCKS,...  16.5 us
    pallas_call x1, Pallas kernels, halo(): pl.pallas_call(halo_kernel, out_shape=jax.ShapeDtypeStruct((2, BLOCKS, RO...  9.19 us
    unnamed x16, local copies, waits for them, and re-layouts  3.86 us

profile of v1, /device:TPU:11, one launch (start us, length us, event | category | flops | bytes accessed | tf_op | source)
XLA Modules:
  0.0 79.0 jit_solution(5451506381546477842)
XLA Ops:
  0.6 0.0 copy-start
  1.4 0.0 copy-start.1
  1.4 1.1 %copy-done.1 = f32[2,192,512]{2,1,0:T(8,128)S(1)} copy-done((f32[2,192,512]{2,1,0:T(8,128)S(1)}, f32[2,192,512]{2,1,0:T(8,128)}, u32[]{:S(2)}) %copy-start.1) | copy-done | bytes 786456
  2.5 0.0 copy-start.2
  2.5 0.0 copy-start.3
  2.5 0.0 copy-start.5
  2.5 0.0 copy-start.6
  2.6 9.2 %halo.1.win = f32[2,4,448,128]{3,2,1,0:T(8,128)S(1)} custom-call(f32[2,192,512]{2,1,0:T(8,128)S(1)} %copy-done.1), custom_call_target="tpu_custom_call" | custom-call | tf_op jit(solution)/shard_map/halo/pallas_call | solution.py:373
  11.7 0.0 copy-done
  11.8 0.0 copy-done.2
  11.8 0.0 copy-done.3
  11.8 0.0 copy-done.5
  11.8 0.0 copy-done.6
  11.8 0.0 copy-start.4
  11.8 1.0 %copy-done.4 = bf16[512,512]{1,0:T(8,128)(2,1)S(1)} copy-done((bf16[512,512]{1,0:T(8,128)(2,1)S(1)}, bf16[512,512]{1,0:T(8,128)(2,1)}, u32[]{:S(2)}) %copy-start.4) | copy-done | bytes 524312
  12.8 16.5 %slots.1 = (f32[2,4,448,128]{3,2,1,0:T(8,128)S(1)}, f32[2,256,256]{2,1,0:T(8,128)S(1)}) custom-call(s32[1]{0:T(128)S(6)} %copy.12.cnt, s32[12]{0:T(128)S(1)} %copy-done.5, s32[12]{0:T(128)S(1)} %copy-done.6, f32[2,4,448,128]{3,2,1,0:T(8,128)S(1)} %halo.1.win, f32[2,256,256]{2,1,0:T(8,128)S(1)} %copy-done.2, bf16[12,256,256]{2,1,0:T(8,128)(2,1)S(1)} %copy-done, ...), custom_call_target="tpu_custom_call" | custom-call | tf_op jit(solution)/shard_map/slots/pallas_call | solution.py:391
  29.3 48.0 %merge.1 = (f32[2,192,512]{2,1,0:T(8,128)S(1)}, f32[2,256,256]{2,1,0:T(8,128)S(1)}) custom-call(f32[2,4,448,128]{3,2,1,0:T(8,128)S(1)} %get-tuple-element.4.grad, f32[2,256,256]{2,1,0:T(8,128)S(1)} %get-tuple-element.5.psum), custom_call_target="tpu_custom_call" | custom-call | tf_op jit(solution)/shard_map/merge/pallas_call | solution.py:408
  77.3 0.9 %copy.13 = f32[2,192,512]{2,1,0:T(8,128)} copy(f32[2,192,512]{2,1,0:T(8,128)S(1)} %get-tuple-element.8) | data formatting | bytes 1572864
  78.2 0.8 %copy.14 = f32[2,256,256]{2,1,0:T(8,128)} copy(f32[2,256,256]{2,1,0:T(8,128)S(1)} %get-tuple-element.9) | data formatting | bytes 1048576
Async XLA Ops:
  0.6 11.1 %copy-start = (bf16[12,256,256]{2,1,0:T(8,128)(2,1)S(1)}, bf16[12,256,256]{2,1,0:T(8,128)(2,1)}, u32[]{:S(2)}) copy-start(bf16[12,256,256]{2,1,0:T(8,128)(2,1)} %meas.1) | copy-start | bytes 4718596
  1.4 1.1 %copy-start.1 = (f32[2,192,512]{2,1,0:T(8,128)S(1)}, f32[2,192,512]{2,1,0:T(8,128)}, u32[]{:S(2)}) copy-start(f32[2,192,512]{2,1,0:T(8,128)} %obj.1) | copy-start | bytes 2359300
  2.5 9.2 %copy-start.2 = (f32[2,256,256]{2,1,0:T(8,128)S(1)}, f32[2,256,256]{2,1,0:T(8,128)}, u32[]{:S(2)}) copy-start(f32[2,256,256]{2,1,0:T(8,128)} %probe.1) | copy-start | bytes 1572868
  2.5 9.2 %copy-start.3 = (bf16[512,512]{1,0:T(8,128)(2,1)S(1)}, bf16[512,512]{1,0:T(8,128)(2,1)}, u32[]{:S(2)}) copy-start(bf16[512,512]{1,0:T(8,128)(2,1)} %constant.5.clone.right) | copy-start | bytes 1572868
  2.5 9.2 %copy-start.5 = (s32[12]{0:T(128)S(1)}, s32[12]{0:T(128)}, u32[]{:S(2)}) copy-start(s32[12]{0:T(128)} %row.1) | copy-start | bytes 148
  2.5 9.2 %copy-start.6 = (s32[12]{0:T(128)S(1)}, s32[12]{0:T(128)}, u32[]{:S(2)}) copy-start(s32[12]{0:T(128)} %col.1) | copy-start | bytes 148
  11.8 1.0 %copy-start.4 = (bf16[512,512]{1,0:T(8,128)(2,1)S(1)}, bf16[512,512]{1,0:T(8,128)(2,1)}, u32[]{:S(2)}) copy-start(bf16[512,512]{1,0:T(8,128)(2,1)} %constant.4.clone.left) | copy-start | bytes 1572868

commit v2 on v1

--- a/solution.py
+++ b/solution.py
@@ -13,6 +13,7 @@
 BR = 192
 NCOLS = 512
 CAP = 12
+GROUP = 6
 LIVE = 1024
 LANES = 128
 BLOCKS = NCOLS // LANES
@@ -120,48 +121,77 @@
         fetch(s).start()
         return carry
 
-    lax.fori_loop(0, n, start, 0)
+    def finish(s, carry):
+        fetch(s).wait()
+        return carry
+
+    lax.fori_loop(0, CAP, start, 0)
     grad[...] = jnp.zeros_like(grad)
     psum[...] = jnp.zeros_like(psum)
     lane = lax.broadcasted_iota(jnp.int32, (W, LANES), 1)
 
-    def body(s, carry):
-        r = row[s]
-        c = col[s]
-        block = jnp.where(c >= LANES, 1, 0)
-        shift = c - LANES * block
-        back = lax.rem(LANES - shift, LANES)
-        ahead = lax.rem(shift, LANES)
-        head = lane < LANES - shift
-
-        def patch(plane):
-            parts = [pltpu.roll(win[plane, block + j, pl.ds(r, W), :], back, 1) for j in range(3)]
-            return jnp.concatenate([jnp.where(head, parts[0], parts[1]), jnp.where(head, parts[1], parts[2])], 1)
-
-        pr, pi = patch(0), patch(1)
-        qr, qi = probe[0], probe[1]
-        exit_wave = jnp.concatenate([qr * pr - qi * pi, qr * pi + qi * pr], 0).astype(BF16)
-        half = dot(left[...], exit_wave).astype(BF16)
-        wave = dot(jnp.concatenate([half[:W], half[W:]], 1), right[...])
-        wr, wi = wave[:, :W], wave[:, W:]
-        fetch(s).wait()
-        excess = wr * wr + wi * wi - mbuf[s].astype(F32)
-        resid = jnp.concatenate([wr * excess, wi * excess], 1).astype(BF16)
-        back_wave = dot(resid, left[...]).astype(BF16)
-        chi = dot(right[...], jnp.concatenate([back_wave[:, :W], back_wave[:, W:]], 0))
-        cr, ci = chi[:W], chi[W:]
-        psum[0] += pr * cr + pi * ci
-        psum[1] += pr * ci - pi * cr
-        tail = lane >= shift
-        for plane, g in enumerate((qr * cr + qi * ci, qr * ci - qi * cr)):
-            g0 = pltpu.roll(g[:, :LANES], ahead, 1)
-            g1 = pltpu.roll(g[:, LANES:], ahead, 1)
-            grad[plane, block, pl.ds(r, W), :] += jnp.where(tail, g0, 0.0)
-            grad[plane, block + 1, pl.ds(r, W), :] += jnp.where(tail, g1, g0)
-            grad[plane, block + 2, pl.ds(r, W), :] += jnp.where(tail, 0.0, g1)
+    def group(i, carry):
+        base = GROUP * i
+        place, patches, half, resid, spread, chi = ({} for _ in range(6))
+
+        def enter(k):
+            s = base + k
+            c = col[s]
+            block = jnp.where(c >= LANES, 1, 0)
+            place[k] = (row[s], block, c - LANES * block)
+            r, block, shift = place[k]
+            back = lax.rem(LANES - shift, LANES)
+            head = lane < LANES - shift
+            patch = []
+            for plane in range(2):
+                parts = [pltpu.roll(win[plane, block + j, pl.ds(r, W), :], back, 1) for j in range(3)]
+                patch.append(
+                    jnp.concatenate([jnp.where(head, parts[0], parts[1]), jnp.where(head, parts[1], parts[2])], 1)
+                )
+            patches[k] = patch
+            pr, pi = patch
+            qr, qi = probe[0], probe[1]
+            exit_wave = jnp.concatenate([qr * pr - qi * pi, qr * pi + qi * pr], 0).astype(BF16)
+            half[k] = dot(left[...], exit_wave).astype(BF16)
+
+        def detect(k):
+            wave = dot(jnp.concatenate([half[k][:W], half[k][W:]], 1), right[...])
+            wr, wi = wave[:, :W], wave[:, W:]
+            live = jnp.where(base + k < n, F32(1.0), F32(0.0))
+            excess = (wr * wr + wi * wi - mbuf[base + k].astype(F32)) * live
+            resid[k] = jnp.concatenate([wr * excess, wi * excess], 1).astype(BF16)
+
+        def over_columns(k):
+            spread[k] = dot(resid[k], left[...]).astype(BF16)
+
+        def over_rows(k):
+            chi[k] = dot(right[...], jnp.concatenate([spread[k][:, :W], spread[k][:, W:]], 0))
+
+        def leave(k):
+            r, block, shift = place[k]
+            ahead = lax.rem(shift, LANES)
+            tail = lane >= shift
+            pr, pi = patches[k]
+            qr, qi = probe[0], probe[1]
+            cr, ci = chi[k][:W], chi[k][W:]
+            psum[0] += pr * cr + pi * ci
+            psum[1] += pr * ci - pi * cr
+            for plane, g in enumerate((qr * cr + qi * ci, qr * ci - qi * cr)):
+                g0 = pltpu.roll(g[:, :LANES], ahead, 1)
+                g1 = pltpu.roll(g[:, LANES:], ahead, 1)
+                grad[plane, block, pl.ds(r, W), :] += jnp.where(tail, g0, 0.0)
+                grad[plane, block + 1, pl.ds(r, W), :] += jnp.where(tail, g1, g0)
+                grad[plane, block + 2, pl.ds(r, W), :] += jnp.where(tail, 0.0, g1)
+
+        stages = (enter, detect, over_columns, over_rows, leave)
+        for t in range(GROUP + len(stages) - 1):
+            for at in reversed(range(len(stages))):
+                if 0 <= t - at < GROUP:
+                    stages[at](t - at)
         return carry
 
-    lax.fori_loop(0, n, body, 0)
+    lax.fori_loop(0, CAP, finish, 0)
+    lax.fori_loop(0, (n + GROUP - 1) // GROUP, group, 0)
 
 
 def merge_kernel(

time: 79.2 us -> 67.6 us (0.85)
  the two profiles are of different devices: /device:TPU:11 before, /device:TPU:1 now
where the time goes in v2:
time: 67.6 us; the launch traced here: 67.5 us
  Pallas kernels  62.1 us (92%)
  local copies, waits for them, and re-layouts  3.86 us (6%)
  between operations  1.49 us (2%)
    pallas_call x1, Pallas kernels, merge(): pl.pallas_call(merge_kernel, out_shape=(jax.ShapeDtypeStruct((2, BR, NCOL...  42.7 us
    pallas_call x1, Pallas kernels, halo(): pl.pallas_call(halo_kernel, out_shape=jax.ShapeDtypeStruct((2, BLOCKS, RO...  10.6 us
    pallas_call x1, Pallas kernels, slots(): pl.pallas_call(slots_kernel, out_shape=(jax.ShapeDtypeStruct((2, BLOCKS,...  8.77 us
    unnamed x16, local copies, waits for them, and re-layouts  3.86 us

profile of v2, /device:TPU:1, one launch (start us, length us, event | category | flops | bytes accessed | tf_op | source)
XLA Modules:
  0.0 67.5 jit_solution(9193779631277057813)
XLA Ops:
  0.6 0.0 copy-start
  1.4 0.0 copy-start.1
  1.4 1.1 %copy-done.1 = f32[2,192,512]{2,1,0:T(8,128)S(1)} copy-done((f32[2,192,512]{2,1,0:T(8,128)S(1)}, f32[2,192,512]{2,1,0:T(8,128)}, u32[]{:S(2)}) %copy-start.1) | copy-done | bytes 786456
  2.5 0.0 copy-start.2
  2.5 0.0 copy-start.3
  2.5 0.0 copy-start.5
  2.5 0.0 copy-start.6
  2.6 10.6 %halo.1.win = f32[2,4,448,128]{3,2,1,0:T(8,128)S(1)} custom-call(f32[2,192,512]{2,1,0:T(8,128)S(1)} %copy-done.1), custom_call_target="tpu_custom_call" | custom-call | tf_op jit(solution)/shard_map/halo/pallas_call | solution.py:403
  13.2 0.0 copy-done
  13.2 0.0 copy-done.2
  13.2 0.0 copy-done.3
  13.2 0.0 copy-done.5
  13.2 0.0 copy-done.6
  13.3 0.0 copy-start.4
  13.3 1.0 %copy-done.4 = bf16[512,512]{1,0:T(8,128)(2,1)S(1)} copy-done((bf16[512,512]{1,0:T(8,128)(2,1)S(1)}, bf16[512,512]{1,0:T(8,128)(2,1)}, u32[]{:S(2)}) %copy-start.4) | copy-done | bytes 524312
  14.3 8.8 %slots.1 = (f32[2,4,448,128]{3,2,1,0:T(8,128)S(1)}, f32[2,256,256]{2,1,0:T(8,128)S(1)}) custom-call(s32[1]{0:T(128)S(6)} %copy.12.cnt, s32[12]{0:T(128)S(1)} %copy-done.5, s32[12]{0:T(128)S(1)} %copy-done.6, f32[2,4,448,128]{3,2,1,0:T(8,128)S(1)} %halo.1.win, f32[2,256,256]{2,1,0:T(8,128)S(1)} %copy-done.2, bf16[12,256,256]{2,1,0:T(8,128)(2,1)S(1)} %copy-done, ...), custom_call_target="tpu_custom_call" | custom-call | tf_op jit(solution)/shard_map/slots/pallas_call | solution.py:421
  23.1 42.7 %merge.1 = (f32[2,192,512]{2,1,0:T(8,128)S(1)}, f32[2,256,256]{2,1,0:T(8,128)S(1)}) custom-call(f32[2,4,448,128]{3,2,1,0:T(8,128)S(1)} %get-tuple-element.4.grad, f32[2,256,256]{2,1,0:T(8,128)S(1)} %get-tuple-element.5.psum), custom_call_target="tpu_custom_call" | custom-call | tf_op jit(solution)/shard_map/merge/pallas_call | solution.py:438
  65.8 0.9 %copy.13 = f32[2,192,512]{2,1,0:T(8,128)} copy(f32[2,192,512]{2,1,0:T(8,128)S(1)} %get-tuple-element.8) | data formatting | bytes 1572864
  66.7 0.8 %copy.14 = f32[2,256,256]{2,1,0:T(8,128)} copy(f32[2,256,256]{2,1,0:T(8,128)S(1)} %get-tuple-element.9) | data formatting | bytes 1048576
Async XLA Ops:
  0.6 12.6 %copy-start = (bf16[12,256,256]{2,1,0:T(8,128)(2,1)S(1)}, bf16[12,256,256]{2,1,0:T(8,128)(2,1)}, u32[]{:S(2)}) copy-start(bf16[12,256,256]{2,1,0:T(8,128)(2,1)} %meas.1) | copy-start | bytes 4718596
  1.4 1.1 %copy-start.1 = (f32[2,192,512]{2,1,0:T(8,128)S(1)}, f32[2,192,512]{2,1,0:T(8,128)}, u32[]{:S(2)}) copy-start(f32[2,192,512]{2,1,0:T(8,128)} %obj.1) | copy-start | bytes 2359300
  2.5 10.7 %copy-start.2 = (f32[2,256,256]{2,1,0:T(8,128)S(1)}, f32[2,256,256]{2,1,0:T(8,128)}, u32[]{:S(2)}) copy-start(f32[2,256,256]{2,1,0:T(8,128)} %probe.1) | copy-start | bytes 1572868
  2.5 10.7 %copy-start.3 = (bf16[512,512]{1,0:T(8,128)(2,1)S(1)}, bf16[512,512]{1,0:T(8,128)(2,1)}, u32[]{:S(2)}) copy-start(bf16[512,512]{1,0:T(8,128)(2,1)} %constant.5.clone.right) | copy-start | bytes 1572868
  2.5 10.7 %copy-start.5 = (s32[12]{0:T(128)S(1)}, s32[12]{0:T(128)}, u32[]{:S(2)}) copy-start(s32[12]{0:T(128)} %row.1) | copy-start | bytes 148
  2.5 10.7 %copy-start.6 = (s32[12]{0:T(128)S(1)}, s32[12]{0:T(128)}, u32[]{:S(2)}) copy-start(s32[12]{0:T(128)} %col.1) | copy-start | bytes 148
  13.3 1.0 %copy-start.4 = (bf16[512,512]{1,0:T(8,128)(2,1)S(1)}, bf16[512,512]{1,0:T(8,128)(2,1)}, u32[]{:S(2)}) copy-start(bf16[512,512]{1,0:T(8,128)(2,1)} %constant.4.clone.left) | copy-start | bytes 1572868

commit v3 on v2

v3 whole, which is shorter than its diff:
```python
import math

import jax
import jax.numpy as jnp
import ml_dtypes
import numpy as np
from jax import lax
from jax.experimental import pallas as pl
from jax.experimental.pallas import tpu as pltpu
from jax.sharding import PartitionSpec as P

W = 256
BR = 192
NCOLS = 512
CAP = 12
GROUP = 6
LIVE = 1024
LANES = 128
BLOCKS = NCOLS // LANES
TAIL = 64
ROWS = 2 * BR + TAIL
OWN = 2 * BR
BELOW = BR + TAIL
CHIP = OWN + BELOW
EXTRA = 16
TINY = 1e-33
FULL = 16000.0
NX, NY, NZ = 4, 4, 8
CHIPS = NY * NZ
BANDS = 2 * CHIPS
F32 = jnp.float32
BF16 = jnp.bfloat16
MESH = pl.DeviceIdType.MESH


def table():
    index = np.arange(W, dtype=np.int32)
    phase = index[:, None] * index[None, :] % W
    angle = phase.astype(np.float32) * np.float32(2.0 * math.pi / W)
    factor = np.float32(1.0 / math.sqrt(W))
    real = (np.cos(angle) * factor).astype(ml_dtypes.bfloat16)
    imag = (-np.sin(angle) * factor).astype(ml_dtypes.bfloat16)
    return np.concatenate([real, imag], 1).astype(np.float32)


def dot(a, b):
    return jnp.dot(a, b, preferred_element_type=F32)


def remote(src, dst, send, recv, device):
    return pltpu.make_async_remote_copy(
        src_ref=src, dst_ref=dst, send_sem=send, recv_sem=recv, device_id=device, device_id_type=MESH
    )


def signal(barrier, device):
    pl.semaphore_signal(barrier, inc=1, device_id=device, device_id_type=MESH)


def halo_kernel(
    obj, table, probe_in, meas_in, row_in, col_in,
    win, left, right, probe, meas, row, col,
    own, waves, low, near, far, send, recv, load,
):
    b = lax.axis_index("band")
    barrier = pltpu.get_barrier_semaphore()
    for step in (1, 2):

        @pl.when(b + step < BANDS)
        def _():
            signal(barrier, {"band": b + step})

    loads = [pltpu.make_async_copy(obj.at[plane], own.at[plane], load.at[plane]) for plane in range(2)]
    rest = ((table, waves), (row_in, row), (col_in, col), (probe_in, probe), (meas_in, meas))
    loads += [pltpu.make_async_copy(src, dst, load.at[2 + i]) for i, (src, dst) in enumerate(rest)]
    for copy in loads:
        copy.start()
    for plane in range(2):
        loads[plane].wait()
        low[plane] = own[plane].astype(BF16)

    def copies(step):
        src, dst = (low, near) if step == 1 else (low.at[:, :TAIL], far)
        return [
            remote(src.at[plane], dst.at[plane], send.at[step - 1, plane], recv.at[step - 1, plane], {"band": b - step})
            for plane in range(2)
        ]

    @pl.when(b > 0)
    def _():
        pl.semaphore_wait(barrier, jnp.minimum(b, 2))

    for step in (1, 2):

        @pl.when(b >= step)
        def _():
            for copy in copies(step):
                copy.start()

    loads[2].wait()
    real, imag = waves[:, :W], waves[:, W:]
    for rows, first, second in ((0, real, imag), (W, -imag, real)):
        right[rows : rows + W, :W] = first.astype(BF16)
        right[rows : rows + W, W:] = second.astype(BF16)
    for rows, first, second in ((0, real, -imag), (W, imag, real)):
        left[rows : rows + W, :W] = first.astype(BF16)
        left[rows : rows + W, W:] = second.astype(BF16)

    def fill(src, top, count):
        for plane in range(2):
            for block in range(BLOCKS):
                win[plane, block, top : top + count] = src[plane, :, block * LANES : (block + 1) * LANES].astype(F32)

    fill(low, 0, BR)
    for step, src, top, count in ((1, near, BR, BR), (2, far, 2 * BR, TAIL)):

        @pl.when(b + step < BANDS)
        def _():
            for copy in copies(step):
                copy.wait_recv()
            fill(src, top, count)

        @pl.when(b + step >= BANDS)
        def _():
            win[:, :, top : top + count] = jnp.zeros((2, BLOCKS, count, LANES), F32)

    for copy in loads[3:]:
        copy.wait()
    for step in (1, 2):

        @pl.when(b >= step)
        def _():
            for copy in copies(step):
                copy.wait_send()


def slots_kernel(cnt, row, col, win, probe, meas, left, right, grad, psum):
    grad[...] = jnp.zeros_like(grad)
    psum[...] = jnp.zeros_like(psum)
    n = cnt[0]
    lane = lax.broadcasted_iota(jnp.int32, (W, LANES), 1)

    def group(i, carry):
        base = GROUP * i
        place, patches, half, resid, spread, chi = ({} for _ in range(6))

        def enter(k):
            s = base + k
            c = col[s]
            block = jnp.where(c >= LANES, 1, 0)
            place[k] = (row[s], block, c - LANES * block)
            r, block, shift = place[k]
            back = lax.rem(LANES - shift, LANES)
            head = lane < LANES - shift
            patch = []
            for plane in range(2):
                parts = [pltpu.roll(win[plane, block + j, pl.ds(r, W), :], back, 1) for j in range(3)]
                patch.append(
                    jnp.concatenate([jnp.where(head, parts[0], parts[1]), jnp.where(head, parts[1], parts[2])], 1)
                )
            patches[k] = patch
            pr, pi = patch
            qr, qi = probe[0], probe[1]
            exit_wave = jnp.concatenate([qr * pr - qi * pi, qr * pi + qi * pr], 0).astype(BF16)
            half[k] = dot(left[...], exit_wave).astype(BF16)

        def detect(k):
            wave = dot(jnp.concatenate([half[k][:W], half[k][W:]], 1), right[...])
            wr, wi = wave[:, :W], wave[:, W:]
            live = jnp.where(base + k < n, F32(1.0), F32(0.0))
            excess = (wr * wr + wi * wi - meas[base + k].astype(F32)) * live
            resid[k] = jnp.concatenate([wr * excess, wi * excess], 1).astype(BF16)

        def over_columns(k):
            spread[k] = dot(resid[k], left[...]).astype(BF16)

        def over_rows(k):
            chi[k] = dot(right[...], jnp.concatenate([spread[k][:, :W], spread[k][:, W:]], 0))

        def leave(k):
            r, block, shift = place[k]
            ahead = lax.rem(shift, LANES)
            tail = lane >= shift
            pr, pi = patches[k]
            qr, qi = probe[0], probe[1]
            cr, ci = chi[k][:W], chi[k][W:]
            psum[0] += pr * cr + pi * ci
            psum[1] += pr * ci - pi * cr
            for plane, g in enumerate((qr * cr + qi * ci, qr * ci - qi * cr)):
                g0 = pltpu.roll(g[:, :LANES], ahead, 1)
                g1 = pltpu.roll(g[:, LANES:], ahead, 1)
                grad[plane, block, pl.ds(r, W), :] += jnp.where(tail, g0, 0.0)
                grad[plane, block + 1, pl.ds(r, W), :] += jnp.where(tail, g1, g0)
                grad[plane, block + 2, pl.ds(r, W), :] += jnp.where(tail, 0.0, g1)

        stages = (enter, detect, over_columns, over_rows, leave)
        for t in range(GROUP + len(stages) - 1):
            for at in reversed(range(len(stages))):
                if 0 <= t - at < GROUP:
                    stages[at](t - at)
        return carry

    lax.fori_loop(0, (n + GROUP - 1) // GROUP, group, 0)


def signed_power(value):
    most = jnp.maximum(jnp.max(jnp.abs(value), axis=0, keepdims=True), F32(TINY))
    return jnp.floor(jnp.log2(most))


def code(value, dst, rows):
    power = signed_power(value)
    scaled = value * (jnp.exp2(-power) * F32(FULL))
    dst[:rows] = jnp.round(scaled).astype(jnp.int32).astype(jnp.int16)
    dst[rows:] = jnp.broadcast_to(power, (EXTRA, LANES)).astype(jnp.int32).astype(jnp.int16)


def decode(src, rows):
    power = src[rows:].astype(jnp.int32).astype(F32)[:1]
    return src[:rows].astype(jnp.int32).astype(F32) * (jnp.exp2(power) * F32(1.0 / FULL))


def merge_kernel(
    grad, psum, out, pout,
    from_core, merged, qa, qb, ra, rb, total, other, all_q,
    pcore, psumc, pxy, pz,
    core_s, core_r, a_s, a_r, b_s, b_r, ag_s, ag_r, pc_s, pc_r, xy_s, xy_r, z_s, z_r,
):
    b = lax.axis_index("band")
    p = lax.axis_index("pos")
    core = lax.rem(b, 2)
    chip = b // 2
    z = lax.rem(chip, NZ)
    y = chip // NZ
    sb = b + 1 - 2 * core
    sib = {"band": sb}

    def at(dx, dy=0, **more):
        device = dict(more)
        if dx:
            device["pos"] = lax.rem(p + dx, NX)
        if dy:
            device["band"] = b + 2 * NZ * (lax.rem(y + dy, NY) - y)
        return device

    xys = [(dx, dy) for dy in range(NY) for dx in range(NX) if dx or dy]
    zdev = [None] + [{"band": b + 2 * (lax.rem(z + d, NZ) - z)} for d in range(1, NZ)]

    barrier = pltpu.get_barrier_semaphore()
    for device in [at(dx, band=sb) for dx in range(NX)] + [at(*d) for d in xys] + zdev[1:]:
        signal(barrier, device)
    for dx in range(NX):

        @pl.when(chip > 0)
        def _():
            signal(barrier, at(dx, band=b - 2))

    pl.semaphore_wait(barrier, NX + NX * NY - 1 + NZ - 1 + NX * jnp.minimum(CHIPS - 1 - chip, 1))

    first = remote(psum.at[1 - core], pcore, pc_s.at[0], pc_r.at[0], sib)
    first.start()
    piece = [lax.rem(p + dx, NX) for dx in range(NX)]
    order = (2, 1, 3, 0)
    to_core = {
        dx: remote(
            grad.at[piece[dx] // 2, 2 * (1 - core) + lax.rem(piece[dx], 2)],
            from_core.at[dx], core_s.at[dx], core_r.at[dx], sib,
        )
        for dx in order
    }
    for dx in order:
        to_core[dx].start()

    first.wait_recv()
    psumc[...] = psum[core] + pcore[...]
    xy_send = []
    for i, (dx, dy) in enumerate(xys):
        rows = pl.ds(16 * (NX * lax.rem(y + dy, NY) + lax.rem(p + dx, NX)), 16)
        xy_send.append(remote(psumc.at[rows], pxy.at[i], xy_s.at[i], xy_r.at[i], at(dx, dy)))
    for copy in xy_send:
        copy.start()

    a_send = {dx: remote(qa.at[dx], ra.at[dx], a_s.at[dx], a_r.at[dx], at(dx)) for dx in (2, 1, 3)}
    b_send = {dx: remote(qb.at[dx], rb.at[dx], b_s.at[dx], b_r.at[dx], at(dx, band=b + 2)) for dx in order}
    for dx in order:
        to_core[dx].wait_recv()
        merged[dx, pl.ds(ROWS * (1 - core), BR), :] = jnp.zeros((BR, LANES), F32)
        merged[dx, pl.ds(BR * core, ROWS), :] = grad[piece[dx] // 2, 2 * core + lax.rem(piece[dx], 2)]
        merged[dx, pl.ds(BR * (1 - core), ROWS), :] += from_core[dx]
        if dx:
            code(merged[dx, :OWN, :], qa.at[dx], OWN)
            a_send[dx].start()
        code(merged[dx, OWN:, :], qb.at[dx], BELOW)

        @pl.when(chip < CHIPS - 1)
        def _():
            b_send[dx].start()

    mine = pl.ds(16 * (NX * y + p), 16)
    for copy in xy_send:
        copy.wait_recv()
    part = psumc[mine, :]
    for i in range(len(xys)):
        part = part + pxy[i]
    pz[z] = part
    z_send = [remote(pz.at[z], pz.at[z], z_s.at[d], z_r.at[d], zdev[d]) for d in range(1, NZ)]
    for copy in z_send:
        copy.start()

    for dx in (1, 3, 2):
        a_send[dx].wait_recv()
    total[...] = merged[0, :OWN, :] + (decode(ra.at[1], OWN) + decode(ra.at[3], OWN) + decode(ra.at[2], OWN))

    @pl.when(chip > 0)
    def _():
        for dx in order:
            b_send[dx].wait_recv()
        total[:BELOW, :] += (decode(rb.at[0], BELOW) + decode(rb.at[1], BELOW)) + (
            decode(rb.at[2], BELOW) + decode(rb.at[3], BELOW)
        )

    slot = NX * core + p
    code(total[pl.ds(BR * (1 - core), BR), :], other, BR)
    code(total[pl.ds(BR * core, BR), :], all_q.at[slot], BR)
    gather = [
        remote(all_q.at[slot], all_q.at[slot], ag_s.at[dx], ag_r.at[dx], at(dx)) for dx in range(1, NX)
    ] + [remote(other, all_q.at[slot], ag_s.at[NX + dx], ag_r.at[NX + dx], at(dx, band=sb)) for dx in range(NX)]
    for copy in gather:
        copy.start()

    for copy in z_send:
        copy.wait_recv()
    part = ((pz[0] + pz[1]) + (pz[2] + pz[3])) + ((pz[4] + pz[5]) + (pz[6] + pz[7]))
    pout[core, mine, :] = part * F32(1.0 / math.sqrt(LIVE))
    xy_back = [
        remote(pout.at[core, mine], pout.at[core, mine], xy_s.at[16 + i], xy_r.at[16 + i], at(dx, dy))
        for i, (dx, dy) in enumerate(xys)
    ]
    for copy in xy_back:
        copy.start()

    for copy in gather:
        copy.wait_recv()
    for c in range(2):
        for j in range(NX):
            block = 2 * c + j % 2
            out[j // 2, :, block * LANES : (block + 1) * LANES] = decode(all_q.at[NX * c + j], BR)

    for copy in xy_back:
        copy.wait_recv()
    last = remote(pout.at[core], pout.at[core], pc_s.at[1], pc_r.at[1], sib)
    last.start()
    last.wait_recv()

    for copy in [first, last] + list(to_core.values()) + xy_send + list(a_send.values()) + z_send + gather + xy_back:
        copy.wait_send()

    @pl.when(chip < CHIPS - 1)
    def _():
        for copy in b_send.values():
            copy.wait_send()


VM = pl.BlockSpec(memory_space=pltpu.VMEM)
SM = pl.BlockSpec(memory_space=pltpu.SMEM)
HBM = pl.BlockSpec(memory_space=pltpu.HBM)
DMA = pltpu.SemaphoreType.DMA


def params(cid=None):
    return pltpu.CompilerParams(vmem_limit_bytes=40 << 20, collective_id=cid, has_side_effects=cid is not None)


def halo(obj, waves, probe, measured, rows, cols):
    return pl.pallas_call(
        halo_kernel,
        out_shape=(
            jax.ShapeDtypeStruct((2, BLOCKS, ROWS, LANES), F32),
            jax.ShapeDtypeStruct((2 * W, 2 * W), BF16),
            jax.ShapeDtypeStruct((2 * W, 2 * W), BF16),
            jax.ShapeDtypeStruct(probe.shape, probe.dtype),
            jax.ShapeDtypeStruct(measured.shape, measured.dtype),
            jax.ShapeDtypeStruct(rows.shape, rows.dtype),
            jax.ShapeDtypeStruct(cols.shape, cols.dtype),
        ),
        in_specs=[HBM] * 6,
        out_specs=(VM, VM, VM, VM, VM, SM, SM),
        scratch_shapes=[
            pltpu.VMEM((2, BR, NCOLS), F32),
            pltpu.VMEM((W, 2 * W), F32),
            pltpu.VMEM((2, BR, NCOLS), BF16),
            pltpu.VMEM((2, BR, NCOLS), BF16),
            pltpu.VMEM((2, TAIL, NCOLS), BF16),
            DMA((2, 2)),
            DMA((2, 2)),
            DMA((7,)),
        ],
        compiler_params=params(0),
        name="halo",
    )(obj, waves, probe, measured, rows, cols)


def slots(counts, rows, cols, win, probe, measured, left, right):
    return pl.pallas_call(
        slots_kernel,
        out_shape=(
            jax.ShapeDtypeStruct((2, BLOCKS, ROWS, LANES), F32),
            jax.ShapeDtypeStruct((2, W, W), F32),
        ),
        in_specs=[SM, SM, SM, VM, VM, VM, VM, VM],
        out_specs=(VM, VM),
        compiler_params=params(),
        name="slots",
    )(counts, rows, cols, win, probe, measured, left, right)


def merge(grad, psum):
    coded = lambda n, *lead: pltpu.VMEM((*lead, n + EXTRA, LANES), jnp.int16)
    piece = lambda n, *lead: pltpu.VMEM((*lead, n, LANES), F32)
    flat = lambda n, *lead: pltpu.VMEM((*lead, n, W), F32)
    return pl.pallas_call(
        merge_kernel,
        out_shape=(
            jax.ShapeDtypeStruct((2, BR, NCOLS), F32),
            jax.ShapeDtypeStruct((2, W, W), F32),
        ),
        in_specs=[VM, VM],
        out_specs=(VM, VM),
        scratch_shapes=[
            piece(ROWS, NX), piece(CHIP, NX),
            coded(OWN, NX), coded(BELOW, NX), coded(OWN, NX), coded(BELOW, NX),
            piece(OWN), coded(BR), coded(BR, 2 * NX),
            flat(W), flat(W), flat(16, 15), flat(16, NZ),
        ]
        + [DMA((NX,))] * 6
        + [DMA((2 * NX,))] * 2
        + [DMA((2,))] * 2
        + [DMA((32,))] * 2
        + [DMA((NZ,))] * 2,
        compiler_params=params(1),
        name="merge",
    )(grad, psum)


def on_device(object_field, probe, measured, row_offset, col_offset, counts):
    win, left, right, probe, measured, rows, cols = halo(
        *[
            pltpu.with_memory_space_constraint(v, pltpu.HBM)
            for v in (object_field, jnp.asarray(table()), probe, measured, row_offset, col_offset)
        ]
    )
    grad, psum = slots(counts, rows, cols, win, probe, measured, left, right)
    return merge(grad, psum)


def solution(mesh):
    placed = (
        P(None, "band", None),
        P(),
        P(("band", "pos"), None, None),
        P(("band", "pos")),
        P(("band", "pos")),
        P(("band", "pos")),
    )
    return jax.shard_map(
        on_device,
        mesh=mesh,
        in_specs=placed,
        out_specs=(P(None, "band", None), P()),
        check_vma=False,
    )
```

time: 67.6 us -> 62.6 us (0.926)
  Pallas kernels: 62.1 us -> 59.5 us
  local copies, waits for them, and re-layouts: 3.86 us -> 1.67 us
    pallas_call x1, Pallas kernels: 8.77 us -> 6.15 us  [slots(): pl.pallas_call(slots_kernel, out_shape=(jax.ShapeDtypeStruct((2, BLOCKS,...]
    unnamed x16 -> x2, local copies, waits for them, and re-layouts: 3.86 us -> 1.67 us
    pallas_call x1, Pallas kernels: 10.6 us -> 11.3 us  [halo(): pl.pallas_call(halo_kernel, out_shape=(jax.ShapeDtypeStruct((2, BLOCKS, R...]
    pallas_call x1, Pallas kernels: 42.7 us -> 42 us  [merge(): pl.pallas_call(merge_kernel, out_shape=(jax.ShapeDtypeStruct((2, BR, NCOL...]
where the time goes in v3:
time: 62.6 us; the launch traced here: 62.5 us
  Pallas kernels  59.5 us (95%)
  local copies, waits for them, and re-layouts  1.67 us (3%)
  between operations  1.3 us (2%)
    pallas_call x1, Pallas kernels, merge(): pl.pallas_call(merge_kernel, out_shape=(jax.ShapeDtypeStruct((2, BR, NCOL...  42 us
    pallas_call x1, Pallas kernels, halo(): pl.pallas_call(halo_kernel, out_shape=(jax.ShapeDtypeStruct((2, BLOCKS, R...  11.3 us
    pallas_call x1, Pallas kernels, slots(): pl.pallas_call(slots_kernel, out_shape=(jax.ShapeDtypeStruct((2, BLOCKS,...  6.15 us
    unnamed x2, local copies, waits for them, and re-layouts  1.67 us

profile of v3, /device:TPU:1, one launch (start us, length us, event | category | flops | bytes accessed | tf_op | source)
XLA Modules:
  0.0 62.5 jit_solution(11877424326271178097)
XLA Ops:
  1.3 11.3 %halo.1 = (f32[2,4,448,128]{3,2,1,0:T(8,128)S(1)}, bf16[512,512]{1,0:T(8,128)(2,1)S(1)}, bf16[512,512]{1,0:T(8,128)(2,1)S(1)}, f32[2,256,256]{2,1,0:T(8,128)S(1)...) custom-call(f32[2,192,512]{2,1,0:T(8,128)} %obj.1, f32[256,512]{1,0:T(8,128)} %constant.2.clone.table, ...), custom_call_target="tpu_custom_call" | custom-call | tf_op jit(solution)/shard_map/halo/pallas_call | solution.py:375
  12.6 6.1 %slots.1 = (f32[2,4,448,128]{3,2,1,0:T(8,128)S(1)}, f32[2,256,256]{2,1,0:T(8,128)S(1)}) custom-call(s32[1]{0:T(128)S(6)} %copy.11.cnt, s32[12]{0:T(128)S(1)} %get-tuple-element.11.row, s32[12]{0:T(128)S(1)} %get-tuple-element.12.col, f32[2,4,448,128]{3,2,1,0:T(8,128)S(1)} %get-tuple-element.13.win, f32[2,256,256]{2,1,0:T(8,128)S(1)} %get-tuple-element.14.probe, ...), custom_call_target="tpu_custom_call" | custom-call | tf_op jit(solution)/shard_map/slots/pallas_call | solution.py:404
  18.8 42.0 %merge.1 = (f32[2,192,512]{2,1,0:T(8,128)S(1)}, f32[2,256,256]{2,1,0:T(8,128)S(1)}) custom-call(f32[2,4,448,128]{3,2,1,0:T(8,128)S(1)} %get-tuple-element.18.grad, f32[2,256,256]{2,1,0:T(8,128)S(1)} %get-tuple-element.19.psum), custom_call_target="tpu_custom_call" | custom-call | tf_op jit(solution)/shard_map/merge/pallas_call | solution.py:421
  60.8 0.9 %copy.12 = f32[2,192,512]{2,1,0:T(8,128)} copy(f32[2,192,512]{2,1,0:T(8,128)S(1)} %get-tuple-element.22) | data formatting | bytes 1572864
  61.7 0.8 %copy.13 = f32[2,256,256]{2,1,0:T(8,128)} copy(f32[2,256,256]{2,1,0:T(8,128)S(1)} %get-tuple-element.23) | data formatting | bytes 1048576

commit v4 on v3

--- a/solution.py
+++ b/solution.py
@@ -134,73 +134,79 @@
                 copy.wait_send()
 
 
+def run_group(base, n, row, col, win, probe, meas, left, right, psum, put):
+    lane = lax.broadcasted_iota(jnp.int32, (W, LANES), 1)
+    place, patches, half, resid, spread, chi = ({} for _ in range(6))
+
+    def enter(k):
+        s = base + k
+        c = col[s]
+        block = jnp.where(c >= LANES, 1, 0)
+        place[k] = (row[s], block, c - LANES * block)
+        r, block, shift = place[k]
+        back = lax.rem(LANES - shift, LANES)
+        head = lane < LANES - shift
+        patch = []
+        for plane in range(2):
+            parts = [pltpu.roll(win[plane, block + j, pl.ds(r, W), :], back, 1) for j in range(3)]
+            patch.append(
+                jnp.concatenate([jnp.where(head, parts[0], parts[1]), jnp.where(head, parts[1], parts[2])], 1)
+            )
+        patches[k] = patch
+        pr, pi = patch
+        qr, qi = probe[0], probe[1]
+        exit_wave = jnp.concatenate([qr * pr - qi * pi, qr * pi + qi * pr], 0).astype(BF16)
+        half[k] = dot(left[...], exit_wave).astype(BF16)
+
+    def detect(k):
+        wave = dot(jnp.concatenate([half[k][:W], half[k][W:]], 1), right[...])
+        wr, wi = wave[:, :W], wave[:, W:]
+        live = jnp.where(base + k < n, F32(1.0), F32(0.0))
+        excess = (wr * wr + wi * wi - meas[base + k].astype(F32)) * live
+        resid[k] = jnp.concatenate([wr * excess, wi * excess], 1).astype(BF16)
+
+    def over_columns(k):
+        spread[k] = dot(resid[k], left[...]).astype(BF16)
+
+    def over_rows(k):
+        chi[k] = dot(right[...], jnp.concatenate([spread[k][:, :W], spread[k][:, W:]], 0))
+
+    def leave(k):
+        r, block, shift = place[k]
+        ahead = lax.rem(shift, LANES)
+        tail = lane >= shift
+        pr, pi = patches[k]
+        qr, qi = probe[0], probe[1]
+        cr, ci = chi[k][:W], chi[k][W:]
+        psum[0] += pr * cr + pi * ci
+        psum[1] += pr * ci - pi * cr
+        for plane, g in enumerate((qr * cr + qi * ci, qr * ci - qi * cr)):
+            g0 = pltpu.roll(g[:, :LANES], ahead, 1)
+            g1 = pltpu.roll(g[:, LANES:], ahead, 1)
+            parts = jnp.where(tail, g0, 0.0), jnp.where(tail, g1, g0), jnp.where(tail, 0.0, g1)
+            put(k, plane, r, block, parts)
+
+    stages = (enter, detect, over_columns, over_rows, leave)
+    for t in range(GROUP + len(stages) - 1):
+        for at in reversed(range(len(stages))):
+            if 0 <= t - at < GROUP:
+                stages[at](t - at)
+
+
 def slots_kernel(cnt, row, col, win, probe, meas, left, right, grad, psum):
     grad[...] = jnp.zeros_like(grad)
     psum[...] = jnp.zeros_like(psum)
     n = cnt[0]
-    lane = lax.broadcasted_iota(jnp.int32, (W, LANES), 1)
+
+    def put(k, plane, r, block, parts):
+        for j, part in enumerate(parts):
+            grad[plane, block + j, pl.ds(r, W), :] += part
 
     def group(i, carry):
-        base = GROUP * i
-        place, patches, half, resid, spread, chi = ({} for _ in range(6))
-
-        def enter(k):
-            s = base + k
-            c = col[s]
-            block = jnp.where(c >= LANES, 1, 0)
-            place[k] = (row[s], block, c - LANES * block)
-            r, block, shift = place[k]
-            back = lax.rem(LANES - shift, LANES)
-            head = lane < LANES - shift
-            patch = []
-            for plane in range(2):
-                parts = [pltpu.roll(win[plane, block + j, pl.ds(r, W), :], back, 1) for j in range(3)]
-                patch.append(
-                    jnp.concatenate([jnp.where(head, parts[0], parts[1]), jnp.where(head, parts[1], parts[2])], 1)
-                )
-            patches[k] = patch
-            pr, pi = patch
-            qr, qi = probe[0], probe[1]
-            exit_wave = jnp.concatenate([qr * pr - qi * pi, qr * pi + qi * pr], 0).astype(BF16)
-            half[k] = dot(left[...], exit_wave).astype(BF16)
-
-        def detect(k):
-            wave = dot(jnp.concatenate([half[k][:W], half[k][W:]], 1), right[...])
-            wr, wi = wave[:, :W], wave[:, W:]
-            live = jnp.where(base + k < n, F32(1.0), F32(0.0))
-            excess = (wr * wr + wi * wi - meas[base + k].astype(F32)) * live
-            resid[k] = jnp.concatenate([wr * excess, wi * excess], 1).astype(BF16)
-
-        def over_columns(k):
-            spread[k] = dot(resid[k], left[...]).astype(BF16)
-
-        def over_rows(k):
-            chi[k] = dot(right[...], jnp.concatenate([spread[k][:, :W], spread[k][:, W:]], 0))
-
-        def leave(k):
-            r, block, shift = place[k]
-            ahead = lax.rem(shift, LANES)
-            tail = lane >= shift
-            pr, pi = patches[k]
-            qr, qi = probe[0], probe[1]
-            cr, ci = chi[k][:W], chi[k][W:]
-            psum[0] += pr * cr + pi * ci
-            psum[1] += pr * ci - pi * cr
-            for plane, g in enumerate((qr * cr + qi * ci, qr * ci - qi * cr)):
-                g0 = pltpu.roll(g[:, :LANES], ahead, 1)
-                g1 = pltpu.roll(g[:, LANES:], ahead, 1)
-                grad[plane, block, pl.ds(r, W), :] += jnp.where(tail, g0, 0.0)
-                grad[plane, block + 1, pl.ds(r, W), :] += jnp.where(tail, g1, g0)
-                grad[plane, block + 2, pl.ds(r, W), :] += jnp.where(tail, 0.0, g1)
-
-        stages = (enter, detect, over_columns, over_rows, leave)
-        for t in range(GROUP + len(stages) - 1):
-            for at in reversed(range(len(stages))):
-                if 0 <= t - at < GROUP:
-                    stages[at](t - at)
+        run_group(GROUP * (i + 1), n, row, col, win, probe, meas, left, right, psum, put)
         return carry
 
-    lax.fori_loop(0, (n + GROUP - 1) // GROUP, group, 0)
+    lax.fori_loop(0, (n - 1) // GROUP, group, 0)
 
 
 def signed_power(value):
@@ -221,8 +227,8 @@
 
 
 def merge_kernel(
-    grad, psum, out, pout,
-    from_core, merged, qa, qb, ra, rb, total, other, all_q,
+    cnt, row, col, win, probe, meas, left, right, grad, psum_in, out, pout,
+    spots, psum, to_core_buf, from_core, merged, qa, qb, ra, rb, total, other, all_q,
     pcore, psumc, pxy, pz,
     core_s, core_r, a_s, a_r, b_s, b_r, ag_s, ag_r, pc_s, pc_r, xy_s, xy_r, z_s, z_r,
 ):
@@ -255,6 +261,27 @@
         def _():
             signal(barrier, at(dx, band=b - 2))
 
+    for k in range(GROUP):
+        spots[k, :, :, :BR, :] = jnp.zeros((2, BLOCKS, BR, LANES), F32)
+        spots[k, :, :, BR + W :, :] = jnp.zeros((2, BLOCKS, BR, LANES), F32)
+    psum[...] = psum_in[...]
+    middle = pl.ds(BR, W)
+
+    def put(k, plane, r, block, parts):
+        second = block > 0
+        a, c, d = parts
+        zero = jnp.zeros_like(a)
+        for j, (low, high) in enumerate(((a, zero), (c, a), (d, c), (zero, d))):
+            spots[k, plane, j, middle, :] = jnp.where(second, high, low)
+
+    run_group(0, cnt[0], row, col, win, probe, meas, left, right, psum, put)
+
+    def window(plane, block):
+        total = grad[plane, block]
+        for k in range(GROUP):
+            total = total + spots[k, plane, block, pl.ds(BR - row[k], ROWS), :]
+        return total
+
     pl.semaphore_wait(barrier, NX + NX * NY - 1 + NZ - 1 + NX * jnp.minimum(CHIPS - 1 - chip, 1))
 
     first = remote(psum.at[1 - core], pcore, pc_s.at[0], pc_r.at[0], sib)
@@ -262,13 +289,10 @@
     piece = [lax.rem(p + dx, NX) for dx in range(NX)]
     order = (2, 1, 3, 0)
     to_core = {
-        dx: remote(
-            grad.at[piece[dx] // 2, 2 * (1 - core) + lax.rem(piece[dx], 2)],
-            from_core.at[dx], core_s.at[dx], core_r.at[dx], sib,
-        )
-        for dx in order
+        dx: remote(to_core_buf.at[dx], from_core.at[dx], core_s.at[dx], core_r.at[dx], sib) for dx in order
     }
     for dx in order:
+        to_core_buf[dx] = window(piece[dx] // 2, 2 * (1 - core) + lax.rem(piece[dx], 2))
         to_core[dx].start()
 
     first.wait_recv()
@@ -283,9 +307,9 @@
     a_send = {dx: remote(qa.at[dx], ra.at[dx], a_s.at[dx], a_r.at[dx], at(dx)) for dx in (2, 1, 3)}
     b_send = {dx: remote(qb.at[dx], rb.at[dx], b_s.at[dx], b_r.at[dx], at(dx, band=b + 2)) for dx in order}
     for dx in order:
+        merged[dx, pl.ds(ROWS * (1 - core), BR), :] = jnp.zeros((BR, LANES), F32)
+        merged[dx, pl.ds(BR * core, ROWS), :] = window(piece[dx] // 2, 2 * core + lax.rem(piece[dx], 2))
         to_core[dx].wait_recv()
-        merged[dx, pl.ds(ROWS * (1 - core), BR), :] = jnp.zeros((BR, LANES), F32)
-        merged[dx, pl.ds(BR * core, ROWS), :] = grad[piece[dx] // 2, 2 * core + lax.rem(piece[dx], 2)]
         merged[dx, pl.ds(BR * (1 - core), ROWS), :] += from_core[dx]
         if dx:
             code(merged[dx, :OWN, :], qa.at[dx], OWN)
@@ -414,7 +438,7 @@
     )(counts, rows, cols, win, probe, measured, left, right)
 
 
-def merge(grad, psum):
+def merge(counts, rows, cols, win, probe, measured, left, right, grad, psum):
     coded = lambda n, *lead: pltpu.VMEM((*lead, n + EXTRA, LANES), jnp.int16)
     piece = lambda n, *lead: pltpu.VMEM((*lead, n, LANES), F32)
     flat = lambda n, *lead: pltpu.VMEM((*lead, n, W), F32)
@@ -424,10 +448,11 @@
             jax.ShapeDtypeStruct((2, BR, NCOLS), F32),
             jax.ShapeDtypeStruct((2, W, W), F32),
         ),
-        in_specs=[VM, VM],
+        in_specs=[SM] * 3 + [VM] * 7,
         out_specs=(VM, VM),
         scratch_shapes=[
-            piece(ROWS, NX), piece(CHIP, NX),
+            piece(W + 2 * BR, GROUP, 2, BLOCKS), flat(W, 2),
+            piece(ROWS, NX), piece(ROWS, NX), piece(CHIP, NX),
             coded(OWN, NX), coded(BELOW, NX), coded(OWN, NX), coded(BELOW, NX),
             piece(OWN), coded(BR), coded(BR, 2 * NX),
             flat(W), flat(W), flat(16, 15), flat(16, NZ),
@@ -439,7 +464,7 @@
         + [DMA((NZ,))] * 2,
         compiler_params=params(1),
         name="merge",
-    )(grad, psum)
+    )(counts, rows, cols, win, probe, measured, left, right, grad, psum)
 
 
 def on_device(object_field, probe, measured, row_offset, col_offset, counts):
@@ -450,7 +475,7 @@
         ]
     )
     grad, psum = slots(counts, rows, cols, win, probe, measured, left, right)
-    return merge(grad, psum)
+    return merge(counts, rows, cols, win, probe, measured, left, right, grad, psum)
 
 
 def solution(mesh):

time: 62.6 us -> 58.6 us (0.936)
  Pallas kernels: 59.5 us -> 55.5 us
    pallas_call x1, Pallas kernels: 42 us -> 38 us  [merge(): pl.pallas_call(merge_kernel, out_shape=(jax.ShapeDtypeStruct((2, BR, NCOL...]
where the time goes in v4:
time: 58.6 us; the launch traced here: 58.5 us
  Pallas kernels  55.5 us (95%)
  local copies, waits for them, and re-layouts  1.67 us (3%)
  between operations  1.3 us (2%)
    pallas_call x1, Pallas kernels, merge(): pl.pallas_call(merge_kernel, out_shape=(jax.ShapeDtypeStruct((2, BR, NCOL...  38 us
    pallas_call x1, Pallas kernels, halo(): pl.pallas_call(halo_kernel, out_shape=(jax.ShapeDtypeStruct((2, BLOCKS, R...  11.3 us
    pallas_call x1, Pallas kernels, slots(): pl.pallas_call(slots_kernel, out_shape=(jax.ShapeDtypeStruct((2, BLOCKS,...  6.12 us
    unnamed x2, local copies, waits for them, and re-layouts  1.67 us

profile of v4, /device:TPU:1, one launch (start us, length us, event | category | flops | bytes accessed | tf_op | source)
XLA Modules:
  0.0 58.5 jit_solution(6719070470874859303)
XLA Ops:
  1.3 11.3 %halo.1 = (f32[2,4,448,128]{3,2,1,0:T(8,128)S(1)}, bf16[512,512]{1,0:T(8,128)(2,1)S(1)}, bf16[512,512]{1,0:T(8,128)(2,1)S(1)}, f32[2,256,256]{2,1,0:T(8,128)S(1)...) custom-call(f32[2,192,512]{2,1,0:T(8,128)} %obj.1, f32[256,512]{1,0:T(8,128)} %constant.2.clone.table, ...), custom_call_target="tpu_custom_call" | custom-call | tf_op jit(solution)/shard_map/halo/pallas_call | solution.py:399
  12.6 6.1 %slots.1 = (f32[2,4,448,128]{3,2,1,0:T(8,128)S(1)}, f32[2,256,256]{2,1,0:T(8,128)S(1)}) custom-call(s32[1]{0:T(128)S(6)} %copy.11.cnt, s32[12]{0:T(128)S(1)} %get-tuple-element.11.row, s32[12]{0:T(128)S(1)} %get-tuple-element.12.col, f32[2,4,448,128]{3,2,1,0:T(8,128)S(1)} %get-tuple-element.13.win, f32[2,256,256]{2,1,0:T(8,128)S(1)} %get-tuple-element.14.probe, ...), custom_call_target="tpu_custom_call" | custom-call | tf_op jit(solution)/shard_map/slots/pallas_call | solution.py:428
  18.8 38.0 %merge.1 = (f32[2,192,512]{2,1,0:T(8,128)S(1)}, f32[2,256,256]{2,1,0:T(8,128)S(1)}) custom-call(s32[1]{0:T(128)S(6)} %copy.11.cnt, s32[12]{0:T(128)S(1)} %get-tuple-element.11.row, s32[12]{0:T(128)S(1)} %get-tuple-element.12.col, f32[2,4,448,128]{3,2,1,0:T(8,128)S(1)} %get-tuple-element.13.win, f32[2,256,256]{2,1,0:T(8,128)S(1)} %get-tuple-element.14.probe, ...), custom_call_target="tpu_custom_call" | custom-call | tf_op jit(solution)/shard_map/merge/pallas_call | solution.py:445
  56.8 0.9 %copy.12 = f32[2,192,512]{2,1,0:T(8,128)} copy(f32[2,192,512]{2,1,0:T(8,128)S(1)} %get-tuple-element.22) | data formatting | bytes 1572864
  57.7 0.8 %copy.13 = f32[2,256,256]{2,1,0:T(8,128)} copy(f32[2,256,256]{2,1,0:T(8,128)S(1)} %get-tuple-element.23) | data formatting | bytes 1048576

commit v5 on v4

--- a/solution.py
+++ b/solution.py
@@ -63,12 +63,16 @@
     own, waves, low, near, far, send, recv, load,
 ):
     b = lax.axis_index("band")
+    odd = lax.rem(b, 2)
     barrier = pltpu.get_barrier_semaphore()
-    for step in (1, 2):
-
-        @pl.when(b + step < BANDS)
-        def _():
-            signal(barrier, {"band": b + step})
+
+    @pl.when(b + 1 < BANDS)
+    def _():
+        signal(barrier, {"band": b + 1})
+
+    @pl.when((odd == 1) & (b + 2 < BANDS))
+    def _():
+        signal(barrier, {"band": b + 2})
 
     loads = [pltpu.make_async_copy(obj.at[plane], own.at[plane], load.at[plane]) for plane in range(2)]
     rest = ((table, waves), (row_in, row), (col_in, col), (probe_in, probe), (meas_in, meas))
@@ -79,23 +83,26 @@
         loads[plane].wait()
         low[plane] = own[plane].astype(BF16)
 
-    def copies(step):
-        src, dst = (low, near) if step == 1 else (low.at[:, :TAIL], far)
-        return [
-            remote(src.at[plane], dst.at[plane], send.at[step - 1, plane], recv.at[step - 1, plane], {"band": b - step})
-            for plane in range(2)
-        ]
+    head, rest_rows = pl.ds(0, TAIL), pl.ds(TAIL, BR - TAIL)
+    above = [
+        remote(low.at[:, rows], near.at[:, rows], send.at[i], recv.at[i], {"band": b - 1})
+        for i, rows in enumerate((head, rest_rows))
+    ]
+    skip = remote(low.at[:, head], far, send.at[2], recv.at[2], {"band": b - 2})
+    relay = remote(near.at[:, head], far, send.at[3], recv.at[2], {"band": b - 1})
 
     @pl.when(b > 0)
     def _():
-        pl.semaphore_wait(barrier, jnp.minimum(b, 2))
-
-    for step in (1, 2):
-
-        @pl.when(b >= step)
-        def _():
-            for copy in copies(step):
-                copy.start()
+        pl.semaphore_wait(barrier, jnp.where((odd == 1) & (b > 2), 2, 1))
+
+    @pl.when((odd == 1) & (b > 2))
+    def _():
+        skip.start()
+
+    @pl.when(b > 0)
+    def _():
+        for copy in above:
+            copy.start()
 
     loads[2].wait()
     real, imag = waves[:, :W], waves[:, W:]
@@ -112,26 +119,47 @@
                 win[plane, block, top : top + count] = src[plane, :, block * LANES : (block + 1) * LANES].astype(F32)
 
     fill(low, 0, BR)
-    for step, src, top, count in ((1, near, BR, BR), (2, far, 2 * BR, TAIL)):
-
-        @pl.when(b + step < BANDS)
+
+    @pl.when(b + 1 < BANDS)
+    def _():
+        above[0].wait_recv()
+
+        @pl.when(odd == 1)
         def _():
-            for copy in copies(step):
-                copy.wait_recv()
-            fill(src, top, count)
-
-        @pl.when(b + step >= BANDS)
-        def _():
-            win[:, :, top : top + count] = jnp.zeros((2, BLOCKS, count, LANES), F32)
+            relay.start()
+
+        fill(near.at[:, head], BR, TAIL)
+        above[1].wait_recv()
+        fill(near.at[:, rest_rows], BR + TAIL, BR - TAIL)
+
+    @pl.when(b + 1 >= BANDS)
+    def _():
+        win[:, :, BR : 2 * BR] = jnp.zeros((2, BLOCKS, BR, LANES), F32)
+
+    @pl.when(b + 2 < BANDS)
+    def _():
+        skip.wait_recv()
+        fill(far, 2 * BR, TAIL)
+
+    @pl.when(b + 2 >= BANDS)
+    def _():
+        win[:, :, 2 * BR :] = jnp.zeros((2, BLOCKS, TAIL, LANES), F32)
 
     for copy in loads[3:]:
         copy.wait()
-    for step in (1, 2):
-
-        @pl.when(b >= step)
-        def _():
-            for copy in copies(step):
-                copy.wait_send()
+
+    @pl.when(b > 0)
+    def _():
+        for copy in above:
+            copy.wait_send()
+
+    @pl.when((odd == 1) & (b > 2))
+    def _():
+        skip.wait_send()
+
+    @pl.when((odd == 1) & (b + 1 < BANDS))
+    def _():
+        relay.wait_send()
 
 
 def run_group(base, n, row, col, win, probe, meas, left, right, psum, put):
@@ -227,8 +255,8 @@
 
 
 def merge_kernel(
-    cnt, row, col, win, probe, meas, left, right, grad, psum_in, out, pout,
-    spots, psum, to_core_buf, from_core, merged, qa, qb, ra, rb, total, other, all_q,
+    cnt, row, col, win, probe, meas, left, right, grad, psum_in, all_q, pout,
+    spots, psum, to_core_buf, from_core, merged, qa, qb, ra, rb, total, other,
     pcore, psumc, pxy, pz,
     core_s, core_r, a_s, a_r, b_s, b_r, ag_s, ag_r, pc_s, pc_r, xy_s, xy_r, z_s, z_r,
 ):
@@ -300,12 +328,12 @@
     xy_send = []
     for i, (dx, dy) in enumerate(xys):
         rows = pl.ds(16 * (NX * lax.rem(y + dy, NY) + lax.rem(p + dx, NX)), 16)
-        xy_send.append(remote(psumc.at[rows], pxy.at[i], xy_s.at[i], xy_r.at[i], at(dx, dy)))
+        xy_send.append(remote(psumc.at[rows], pxy.at[i], xy_s.at[0], xy_r.at[0], at(dx, dy)))
     for copy in xy_send:
         copy.start()
 
-    a_send = {dx: remote(qa.at[dx], ra.at[dx], a_s.at[dx], a_r.at[dx], at(dx)) for dx in (2, 1, 3)}
-    b_send = {dx: remote(qb.at[dx], rb.at[dx], b_s.at[dx], b_r.at[dx], at(dx, band=b + 2)) for dx in order}
+    a_send = {dx: remote(qa.at[dx], ra.at[dx], a_s.at[0], a_r.at[0], at(dx)) for dx in (2, 1, 3)}
+    b_send = {dx: remote(qb.at[dx], rb.at[dx], b_s.at[0], b_r.at[0], at(dx, band=b + 2)) for dx in order}
     for dx in order:
         merged[dx, pl.ds(ROWS * (1 - core), BR), :] = jnp.zeros((BR, LANES), F32)
         merged[dx, pl.ds(BR * core, ROWS), :] = window(piece[dx] // 2, 2 * core + lax.rem(piece[dx], 2))
@@ -321,24 +349,26 @@
             b_send[dx].start()
 
     mine = pl.ds(16 * (NX * y + p), 16)
-    for copy in xy_send:
-        copy.wait_recv()
+    xy_all = remote(pxy, pxy, xy_s.at[0], xy_r.at[0], sib)
+    xy_all.wait_recv()
     part = psumc[mine, :]
     for i in range(len(xys)):
         part = part + pxy[i]
     pz[z] = part
-    z_send = [remote(pz.at[z], pz.at[z], z_s.at[d], z_r.at[d], zdev[d]) for d in range(1, NZ)]
+    z_send = [remote(pz.at[z], pz.at[z], z_s.at[0], z_r.at[0], zdev[d]) for d in range(1, NZ)]
     for copy in z_send:
         copy.start()
 
-    for dx in (1, 3, 2):
-        a_send[dx].wait_recv()
+    for copy in [first, xy_all] + list(to_core.values()):
+        copy.wait_send()
+    a_all = remote(ra.at[pl.ds(1, NX - 1)], ra.at[pl.ds(1, NX - 1)], a_s.at[0], a_r.at[0], sib)
+    b_all = remote(rb, rb, b_s.at[0], b_r.at[0], sib)
+    a_all.wait_recv()
     total[...] = merged[0, :OWN, :] + (decode(ra.at[1], OWN) + decode(ra.at[3], OWN) + decode(ra.at[2], OWN))
 
     @pl.when(chip > 0)
     def _():
-        for dx in order:
-            b_send[dx].wait_recv()
+        b_all.wait_recv()
         total[:BELOW, :] += (decode(rb.at[0], BELOW) + decode(rb.at[1], BELOW)) + (
             decode(rb.at[2], BELOW) + decode(rb.at[3], BELOW)
         )
@@ -346,43 +376,54 @@
     slot = NX * core + p
     code(total[pl.ds(BR * (1 - core), BR), :], other, BR)
     code(total[pl.ds(BR * core, BR), :], all_q.at[slot], BR)
-    gather = [
-        remote(all_q.at[slot], all_q.at[slot], ag_s.at[dx], ag_r.at[dx], at(dx)) for dx in range(1, NX)
-    ] + [remote(other, all_q.at[slot], ag_s.at[NX + dx], ag_r.at[NX + dx], at(dx, band=sb)) for dx in range(NX)]
+    gather = [remote(all_q.at[slot], all_q.at[slot], ag_s.at[0], ag_r.at[0], at(dx)) for dx in range(1, NX)]
+    gather += [remote(other, all_q.at[slot], ag_s.at[0], ag_r.at[0], at(dx, band=sb)) for dx in range(NX)]
     for copy in gather:
         copy.start()
 
-    for copy in z_send:
-        copy.wait_recv()
+    z_all = remote(pz.at[pl.ds(0, NZ - 1)], pz.at[pl.ds(0, NZ - 1)], z_s.at[0], z_r.at[0], sib)
+    z_all.wait_recv()
     part = ((pz[0] + pz[1]) + (pz[2] + pz[3])) + ((pz[4] + pz[5]) + (pz[6] + pz[7]))
     pout[core, mine, :] = part * F32(1.0 / math.sqrt(LIVE))
     xy_back = [
-        remote(pout.at[core, mine], pout.at[core, mine], xy_s.at[16 + i], xy_r.at[16 + i], at(dx, dy))
+        remote(pout.at[core, mine], pout.at[core, mine], xy_s.at[1], xy_r.at[1], at(dx, dy))
         for i, (dx, dy) in enumerate(xys)
     ]
     for copy in xy_back:
         copy.start()
 
-    for copy in gather:
-        copy.wait_recv()
-    for c in range(2):
-        for j in range(NX):
-            block = 2 * c + j % 2
-            out[j // 2, :, block * LANES : (block + 1) * LANES] = decode(all_q.at[NX * c + j], BR)
-
-    for copy in xy_back:
-        copy.wait_recv()
+    for copy in (z_all, a_all):
+        copy.wait_send()
+
+    @pl.when(chip < CHIPS - 1)
+    def _():
+        b_all.wait_send()
+
+    back_all = remote(pxy, pxy, xy_s.at[1], xy_r.at[1], sib)
+    back_all.wait_recv()
     last = remote(pout.at[core], pout.at[core], pc_s.at[1], pc_r.at[1], sib)
     last.start()
-    last.wait_recv()
-
-    for copy in [first, last] + list(to_core.values()) + xy_send + list(a_send.values()) + z_send + gather + xy_back:
+    gather_all = remote(all_q.at[pl.ds(0, 2 * NX - 1)], all_q.at[pl.ds(0, 2 * NX - 1)], ag_s.at[0], ag_r.at[0], sib)
+    gather_all.wait_recv()
+    for copy in (gather_all, back_all):
         copy.wait_send()
-
-    @pl.when(chip < CHIPS - 1)
-    def _():
-        for copy in b_send.values():
-            copy.wait_send()
+    last.wait()
+
+
+def finish_kernel(all_q, psum, out, pout, buf, sems):
+    probe_copy = pltpu.make_async_copy(psum, pout, sems.at[2])
+    probe_copy.start()
+    copies = []
+    for plane in range(2):
+        for c in range(2):
+            for j in range(2):
+                block = 2 * c + j
+                cols = slice(block * LANES, (block + 1) * LANES)
+                buf[plane, :, cols] = decode(all_q.at[NX * c + 2 * plane + j], BR)
+        copies.append(pltpu.make_async_copy(buf.at[plane], out.at[plane], sems.at[plane]))
+        copies[plane].start()
+    for copy in copies + [probe_copy]:
+        copy.wait()
 
 
 VM = pl.BlockSpec(memory_space=pltpu.VMEM)
@@ -415,8 +456,8 @@
             pltpu.VMEM((2, BR, NCOLS), BF16),
             pltpu.VMEM((2, BR, NCOLS), BF16),
             pltpu.VMEM((2, TAIL, NCOLS), BF16),
-            DMA((2, 2)),
-            DMA((2, 2)),
+            DMA((4,)),
+            DMA((3,)),
             DMA((7,)),
         ],
         compiler_params=params(0),
@@ -445,7 +486,7 @@
     return pl.pallas_call(
         merge_kernel,
         out_shape=(
-            jax.ShapeDtypeStruct((2, BR, NCOLS), F32),
+            jax.ShapeDtypeStruct((2 * NX, BR + EXTRA, LANES), jnp.int16),
             jax.ShapeDtypeStruct((2, W, W), F32),
         ),
         in_specs=[SM] * 3 + [VM] * 7,
@@ -454,17 +495,31 @@
             piece(W + 2 * BR, GROUP, 2, BLOCKS), flat(W, 2),
             piece(ROWS, NX), piece(ROWS, NX), piece(CHIP, NX),
             coded(OWN, NX), coded(BELOW, NX), coded(OWN, NX), coded(BELOW, NX),
-            piece(OWN), coded(BR), coded(BR, 2 * NX),
+            piece(OWN), coded(BR),
             flat(W), flat(W), flat(16, 15), flat(16, NZ),
         ]
-        + [DMA((NX,))] * 6
-        + [DMA((2 * NX,))] * 2
-        + [DMA((2,))] * 2
-        + [DMA((32,))] * 2
-        + [DMA((NZ,))] * 2,
+        + [DMA((NX,))] * 2
+        + [DMA((1,))] * 6
+        + [DMA((2,))] * 4
+        + [DMA((1,))] * 2,
         compiler_params=params(1),
         name="merge",
     )(counts, rows, cols, win, probe, measured, left, right, grad, psum)
+
+
+def finish(all_q, psum):
+    return pl.pallas_call(
+        finish_kernel,
+        out_shape=(
+            jax.ShapeDtypeStruct((2, BR, NCOLS), F32),
+            jax.ShapeDtypeStruct((2, W, W), F32),
+        ),
+        in_specs=[VM, VM],
+        out_specs=(HBM, HBM),
+        scratch_shapes=[pltpu.VMEM((2, BR, NCOLS), F32), DMA((3,))],
+        compiler_params=params(),
+        name="finish",
+    )(all_q, psum)
 
 
 def on_device(object_field, probe, measured, row_offset, col_offset, counts):
@@ -475,7 +530,7 @@
         ]
     )
     grad, psum = slots(counts, rows, cols, win, probe, measured, left, right)
-    return merge(counts, rows, cols, win, probe, measured, left, right, grad, psum)
+    return finish(*merge(counts, rows, cols, win, probe, measured, left, right, grad, psum))
 
 
 def solution(mesh):

time: 58.6 us -> 56.1 us (0.957)
  local copies, waits for them, and re-layouts: 1.67 us -> 0 us
  Pallas kernels: 55.5 us -> 54.5 us
    pallas_call x1, Pallas kernels: 6.12 us -> 0.7 us  [slots(): pl.pallas_call(slots_kernel, out_shape=(jax.ShapeDtypeStruct((2, BLOCKS,...]
    pallas_call x1 -> x2, Pallas kernels: 38 us -> 42.7 us  [the longest x1 41.6 us: merge(): pl.pallas_call(merge_kernel, out_shape=(jax.ShapeDtypeStruct((2 * NX, BR...]
    unnamed x2 -> x0, local copies, waits for them, and re-layouts: 1.67 us -> none
where the time goes in v5:
time: 56.1 us; the launch traced here: 56 us
  Pallas kernels  54.5 us (97%)
  between operations  1.46 us (3%)
    pallas_call x1, Pallas kernels, merge(): pl.pallas_call(merge_kernel, out_shape=(jax.ShapeDtypeStruct((2 * NX, BR...  41.6 us
    pallas_call x1, Pallas kernels, halo(): pl.pallas_call(halo_kernel, out_shape=(jax.ShapeDtypeStruct((2, BLOCKS, R...  11.2 us

profile of v5, /device:TPU:1, one launch (start us, length us, event | category | flops | bytes accessed | tf_op | source)
XLA Modules:
  0.0 56.0 jit_solution(1704056145035410212)
XLA Ops:
  1.3 11.2 %halo.1 = (f32[2,4,448,128]{3,2,1,0:T(8,128)S(1)}, bf16[512,512]{1,0:T(8,128)(2,1)S(1)}, bf16[512,512]{1,0:T(8,128)(2,1)S(1)}, f32[2,256,256]{2,1,0:T(8,128)S(1)...) custom-call(f32[2,192,512]{2,1,0:T(8,128)} %obj.1, f32[256,512]{1,0:T(8,128)} %constant.2.clone.table, ...), custom_call_target="tpu_custom_call" | custom-call | tf_op jit(solution)/shard_map/halo/pallas_call | solution.py:440
  12.4 0.7 %slots.1 = (f32[2,4,448,128]{3,2,1,0:T(8,128)S(1)}, f32[2,256,256]{2,1,0:T(8,128)S(1)}) custom-call(s32[1]{0:T(128)S(6)} %copy.9.cnt, s32[12]{0:T(128)S(1)} %get-tuple-element.13.row, s32[12]{0:T(128)S(1)} %get-tuple-element.14.col, f32[2,4,448,128]{3,2,1,0:T(8,128)S(1)} %get-tuple-element.15.win, f32[2,256,256]{2,1,0:T(8,128)S(1)} %get-tuple-element.16.probe, ...), custom_call_target="tpu_custom_call" | custom-call | tf_op jit(solution)/shard_map/slots/pallas_call | solution.py:469
  13.2 41.6 %merge.1 = (s16[8,208,128]{2,1,0:T(8,128)(2,1)S(1)}, f32[2,256,256]{2,1,0:T(8,128)S(1)}) custom-call(s32[1]{0:T(128)S(6)} %copy.9.cnt, s32[12]{0:T(128)S(1)} %get-tuple-element.13.row, s32[12]{0:T(128)S(1)} %get-tuple-element.14.col, f32[2,4,448,128]{3,2,1,0:T(8,128)S(1)} %get-tuple-element.15.win, f32[2,256,256]{2,1,0:T(8,128)S(1)} %get-tuple-element.16.probe, ...), custom_call_target="tpu_custom_call" | custom-call | tf_op jit(solution)/shard_map/merge/pallas_call | solution.py:486
  54.8 1.1 %finish.1 = (f32[2,192,512]{2,1,0:T(8,128)}, f32[2,256,256]{2,1,0:T(8,128)}) custom-call(s16[8,208,128]{2,1,0:T(8,128)(2,1)S(1)} %get-tuple-element.22.all_q, f32[2,256,256]{2,1,0:T(8,128)S(1)} %get-tuple-element.23.psum), custom_call_target="tpu_custom_call" | custom-call | tf_op jit(solution)/shard_map/finish/pallas_call | solution.py:511

commit v6 on v5

--- a/solution.py
+++ b/solution.py
@@ -249,16 +249,17 @@
     dst[rows:] = jnp.broadcast_to(power, (EXTRA, LANES)).astype(jnp.int32).astype(jnp.int16)
 
 
-def decode(src, rows):
+def decode(src, rows, first=0, last=None):
+    last = rows if last is None else last
     power = src[rows:].astype(jnp.int32).astype(F32)[:1]
-    return src[:rows].astype(jnp.int32).astype(F32) * (jnp.exp2(power) * F32(1.0 / FULL))
+    return src[first:last].astype(jnp.int32).astype(F32) * (jnp.exp2(power) * F32(1.0 / FULL))
 
 
 def merge_kernel(
     cnt, row, col, win, probe, meas, left, right, grad, psum_in, all_q, pout,
-    spots, psum, to_core_buf, from_core, merged, qa, qb, ra, rb, total, other,
+    spots, psum, to_core_buf, from_core, merged, qa, qb, ra, rb, qs, rs, total, other,
     pcore, psumc, pxy, pz,
-    core_s, core_r, a_s, a_r, b_s, b_r, ag_s, ag_r, pc_s, pc_r, xy_s, xy_r, z_s, z_r,
+    core_s, core_r, a_s, a_r, b_s, b_r, sh_s, sh_r, ag_s, ag_r, pc_s, pc_r, xy_s, xy_r, z_s, z_r,
 ):
     b = lax.axis_index("band")
     p = lax.axis_index("pos")
@@ -283,11 +284,9 @@
     barrier = pltpu.get_barrier_semaphore()
     for device in [at(dx, band=sb) for dx in range(NX)] + [at(*d) for d in xys] + zdev[1:]:
         signal(barrier, device)
-    for dx in range(NX):
-
-        @pl.when(chip > 0)
-        def _():
-            signal(barrier, at(dx, band=b - 2))
+    @pl.when(chip > 0)
+    def _():
+        signal(barrier, {"band": b - 2})
 
     for k in range(GROUP):
         spots[k, :, :, :BR, :] = jnp.zeros((2, BLOCKS, BR, LANES), F32)
@@ -310,7 +309,7 @@
             total = total + spots[k, plane, block, pl.ds(BR - row[k], ROWS), :]
         return total
 
-    pl.semaphore_wait(barrier, NX + NX * NY - 1 + NZ - 1 + NX * jnp.minimum(CHIPS - 1 - chip, 1))
+    pl.semaphore_wait(barrier, NX + NX * NY - 1 + NZ - 1 + jnp.minimum(CHIPS - 1 - chip, 1))
 
     first = remote(psum.at[1 - core], pcore, pc_s.at[0], pc_r.at[0], sib)
     first.start()
@@ -333,20 +332,19 @@
         copy.start()
 
     a_send = {dx: remote(qa.at[dx], ra.at[dx], a_s.at[0], a_r.at[0], at(dx)) for dx in (2, 1, 3)}
-    b_send = {dx: remote(qb.at[dx], rb.at[dx], b_s.at[0], b_r.at[0], at(dx, band=b + 2)) for dx in order}
+    b_send = {dx: remote(qb.at[dx], rb.at[dx], b_s.at[0], b_r.at[0], at(dx)) for dx in (2, 1, 3)}
+    shift = remote(qs, rs, sh_s.at[0], sh_r.at[0], {"band": b + 2})
     for dx in order:
         merged[dx, pl.ds(ROWS * (1 - core), BR), :] = jnp.zeros((BR, LANES), F32)
         merged[dx, pl.ds(BR * core, ROWS), :] = window(piece[dx] // 2, 2 * core + lax.rem(piece[dx], 2))
         to_core[dx].wait_recv()
         merged[dx, pl.ds(BR * (1 - core), ROWS), :] += from_core[dx]
         if dx:
-            code(merged[dx, :OWN, :], qa.at[dx], OWN)
-            a_send[dx].start()
-        code(merged[dx, OWN:, :], qb.at[dx], BELOW)
-
-        @pl.when(chip < CHIPS - 1)
-        def _():
+            code(merged[dx, OWN:, :], qb.at[dx], BELOW)
             b_send[dx].start()
+    for dx in order[:3]:
+        code(merged[dx, :OWN, :], qa.at[dx], OWN)
+        a_send[dx].start()
 
     mine = pl.ds(16 * (NX * y + p), 16)
     xy_all = remote(pxy, pxy, xy_s.at[0], xy_r.at[0], sib)
@@ -361,25 +359,19 @@
 
     for copy in [first, xy_all] + list(to_core.values()):
         copy.wait_send()
-    a_all = remote(ra.at[pl.ds(1, NX - 1)], ra.at[pl.ds(1, NX - 1)], a_s.at[0], a_r.at[0], sib)
-    b_all = remote(rb, rb, b_s.at[0], b_r.at[0], sib)
+    others = pl.ds(1, NX - 1)
+    a_all = remote(ra.at[others], ra.at[others], a_s.at[0], a_r.at[0], sib)
+    b_all = remote(rb.at[others], rb.at[others], b_s.at[0], b_r.at[0], sib)
+    b_all.wait_recv()
+    below = merged[0, OWN:, :] + (decode(rb.at[1], BELOW) + decode(rb.at[3], BELOW) + decode(rb.at[2], BELOW))
+    code(below, qs, BELOW)
+
+    @pl.when(chip < CHIPS - 1)
+    def _():
+        shift.start()
+
     a_all.wait_recv()
     total[...] = merged[0, :OWN, :] + (decode(ra.at[1], OWN) + decode(ra.at[3], OWN) + decode(ra.at[2], OWN))
-
-    @pl.when(chip > 0)
-    def _():
-        b_all.wait_recv()
-        total[:BELOW, :] += (decode(rb.at[0], BELOW) + decode(rb.at[1], BELOW)) + (
-            decode(rb.at[2], BELOW) + decode(rb.at[3], BELOW)
-        )
-
-    slot = NX * core + p
-    code(total[pl.ds(BR * (1 - core), BR), :], other, BR)
-    code(total[pl.ds(BR * core, BR), :], all_q.at[slot], BR)
-    gather = [remote(all_q.at[slot], all_q.at[slot], ag_s.at[0], ag_r.at[0], at(dx)) for dx in range(1, NX)]
-    gather += [remote(other, all_q.at[slot], ag_s.at[0], ag_r.at[0], at(dx, band=sb)) for dx in range(NX)]
-    for copy in gather:
-        copy.start()
 
     z_all = remote(pz.at[pl.ds(0, NZ - 1)], pz.at[pl.ds(0, NZ - 1)], z_s.at[0], z_r.at[0], sib)
     z_all.wait_recv()
@@ -392,12 +384,25 @@
     for copy in xy_back:
         copy.start()
 
-    for copy in (z_all, a_all):
+    @pl.when(chip > 0)
+    def _():
+        shift.wait_recv()
+        total[:BELOW, :] += decode(rs, BELOW)
+
+    slot = NX * core + p
+    code(total[pl.ds(BR * (1 - core), BR), :], other, BR)
+    code(total[pl.ds(BR * core, BR), :], all_q.at[slot], BR)
+    gather = [remote(all_q.at[slot], all_q.at[slot], ag_s.at[0], ag_r.at[0], at(dx)) for dx in range(1, NX)]
+    gather += [remote(other, all_q.at[slot], ag_s.at[0], ag_r.at[0], at(dx, band=sb)) for dx in range(NX)]
+    for copy in gather:
+        copy.start()
+
+    for copy in (z_all, a_all, b_all):
         copy.wait_send()
 
     @pl.when(chip < CHIPS - 1)
     def _():
-        b_all.wait_send()
+        shift.wait_send()
 
     back_all = remote(pxy, pxy, xy_s.at[1], xy_r.at[1], sib)
     back_all.wait_recv()
@@ -494,12 +499,12 @@
         scratch_shapes=[
             piece(W + 2 * BR, GROUP, 2, BLOCKS), flat(W, 2),
             piece(ROWS, NX), piece(ROWS, NX), piece(CHIP, NX),
-            coded(OWN, NX), coded(BELOW, NX), coded(OWN, NX), coded(BELOW, NX),
+            coded(OWN, NX), coded(BELOW, NX), coded(OWN, NX), coded(BELOW, NX), coded(BELOW), coded(BELOW),
             piece(OWN), coded(BR),
             flat(W), flat(W), flat(16, 15), flat(16, NZ),
         ]
         + [DMA((NX,))] * 2
-        + [DMA((1,))] * 6
+        + [DMA((1,))] * 8
         + [DMA((2,))] * 4
         + [DMA((1,))] * 2,
         compiler_params=params(1),

time: 56.1 us -> 53.6 us (0.955)
  Pallas kernels: 54.5 us -> 52 us
    pallas_call x1, Pallas kernels: 41.6 us -> 39.1 us  [merge(): pl.pallas_call(merge_kernel, out_shape=(jax.ShapeDtypeStruct((2 * NX, BR...]
where the time goes in v6:
time: 53.6 us; the launch traced here: 53.5 us
  Pallas kernels  52 us (97%)
  between operations  1.46 us (3%)
    pallas_call x1, Pallas kernels, merge(): pl.pallas_call(merge_kernel, out_shape=(jax.ShapeDtypeStruct((2 * NX, BR...  39.1 us
    pallas_call x1, Pallas kernels, halo(): pl.pallas_call(halo_kernel, out_shape=(jax.ShapeDtypeStruct((2, BLOCKS, R...  11.2 us
    pallas_call x1, Pallas kernels, finish(): pl.pallas_call(finish_kernel, out_shape=(jax.ShapeDtypeStruct((2, BR, NCO...  1.08 us

profile of v6, /device:TPU:1, one launch (start us, length us, event | category | flops | bytes accessed | tf_op | source)
XLA Modules:
  0.0 53.5 jit_solution(3009442617656413361)
XLA Ops:
  1.3 11.2 %halo.1 = (f32[2,4,448,128]{3,2,1,0:T(8,128)S(1)}, bf16[512,512]{1,0:T(8,128)(2,1)S(1)}, bf16[512,512]{1,0:T(8,128)(2,1)S(1)}, f32[2,256,256]{2,1,0:T(8,128)S(1)...) custom-call(f32[2,192,512]{2,1,0:T(8,128)} %obj.1, f32[256,512]{1,0:T(8,128)} %constant.2.clone.table, ...), custom_call_target="tpu_custom_call" | custom-call | tf_op jit(solution)/shard_map/halo/pallas_call | solution.py:445
  12.4 0.7 %slots.1 = (f32[2,4,448,128]{3,2,1,0:T(8,128)S(1)}, f32[2,256,256]{2,1,0:T(8,128)S(1)}) custom-call(s32[1]{0:T(128)S(6)} %copy.9.cnt, s32[12]{0:T(128)S(1)} %get-tuple-element.13.row, s32[12]{0:T(128)S(1)} %get-tuple-element.14.col, f32[2,4,448,128]{3,2,1,0:T(8,128)S(1)} %get-tuple-element.15.win, f32[2,256,256]{2,1,0:T(8,128)S(1)} %get-tuple-element.16.probe, ...), custom_call_target="tpu_custom_call" | custom-call | tf_op jit(solution)/shard_map/slots/pallas_call | solution.py:474
  13.2 39.1 %merge.1 = (s16[8,208,128]{2,1,0:T(8,128)(2,1)S(1)}, f32[2,256,256]{2,1,0:T(8,128)S(1)}) custom-call(s32[1]{0:T(128)S(6)} %copy.9.cnt, s32[12]{0:T(128)S(1)} %get-tuple-element.13.row, s32[12]{0:T(128)S(1)} %get-tuple-element.14.col, f32[2,4,448,128]{3,2,1,0:T(8,128)S(1)} %get-tuple-element.15.win, f32[2,256,256]{2,1,0:T(8,128)S(1)} %get-tuple-element.16.probe, ...), custom_call_target="tpu_custom_call" | custom-call | tf_op jit(solution)/shard_map/merge/pallas_call | solution.py:491
  52.3 1.1 %finish.1 = (f32[2,192,512]{2,1,0:T(8,128)}, f32[2,256,256]{2,1,0:T(8,128)}) custom-call(s16[8,208,128]{2,1,0:T(8,128)(2,1)S(1)} %get-tuple-element.22.all_q, f32[2,256,256]{2,1,0:T(8,128)S(1)} %get-tuple-element.23.psum), custom_call_target="tpu_custom_call" | custom-call | tf_op jit(solution)/shard_map/finish/pallas_call | solution.py:516

commit v7 on v6

--- a/solution.py
+++ b/solution.py
@@ -278,7 +278,9 @@
             device["band"] = b + 2 * NZ * (lax.rem(y + dy, NY) - y)
         return device
 
+    hops = (0, 1, 2, 1)
     xys = [(dx, dy) for dy in range(NY) for dx in range(NX) if dx or dy]
+    xys.sort(key=lambda d: -hops[d[0]] - hops[d[1]])
     zdev = [None] + [{"band": b + 2 * (lax.rem(z + d, NZ) - z)} for d in range(1, NZ)]
 
     barrier = pltpu.get_barrier_semaphore()
@@ -353,7 +355,7 @@
     for i in range(len(xys)):
         part = part + pxy[i]
     pz[z] = part
-    z_send = [remote(pz.at[z], pz.at[z], z_s.at[0], z_r.at[0], zdev[d]) for d in range(1, NZ)]
+    z_send = [remote(pz.at[z], pz.at[z], z_s.at[0], z_r.at[0], zdev[d]) for d in (4, 3, 5, 2, 6, 1, 7)]
     for copy in z_send:
         copy.start()
 
@@ -392,8 +394,11 @@
     slot = NX * core + p
     code(total[pl.ds(BR * (1 - core), BR), :], other, BR)
     code(total[pl.ds(BR * core, BR), :], all_q.at[slot], BR)
-    gather = [remote(all_q.at[slot], all_q.at[slot], ag_s.at[0], ag_r.at[0], at(dx)) for dx in range(1, NX)]
-    gather += [remote(other, all_q.at[slot], ag_s.at[0], ag_r.at[0], at(dx, band=sb)) for dx in range(NX)]
+    gather = []
+    for dx in order:
+        gather.append(remote(other, all_q.at[slot], ag_s.at[0], ag_r.at[0], at(dx, band=sb)))
+        if dx:
+            gather.append(remote(all_q.at[slot], all_q.at[slot], ag_s.at[0], ag_r.at[0], at(dx)))
     for copy in gather:
         copy.start()
 

time: 53.6 us -> 52.4 us (0.978)
  Pallas kernels: 52 us -> 51.1 us
    pallas_call x1, Pallas kernels: 39.1 us -> 38.2 us  [merge(): pl.pallas_call(merge_kernel, out_shape=(jax.ShapeDtypeStruct((2 * NX, BR...]
where the time goes in v7:
time: 52.4 us; the launch traced here: 52.6 us
  Pallas kernels  51.1 us (98%)
  between operations  1.46 us (3%)
    pallas_call x1, Pallas kernels, merge(): pl.pallas_call(merge_kernel, out_shape=(jax.ShapeDtypeStruct((2 * NX, BR...  38.2 us
    pallas_call x1, Pallas kernels, halo(): pl.pallas_call(halo_kernel, out_shape=(jax.ShapeDtypeStruct((2, BLOCKS, R...  11.2 us
    pallas_call x1, Pallas kernels, finish(): pl.pallas_call(finish_kernel, out_shape=(jax.ShapeDtypeStruct((2, BR, NCO...  1.08 us

profile of v7, /device:TPU:1, one launch (start us, length us, event | category | flops | bytes accessed | tf_op | source)
XLA Modules:
  0.0 52.6 jit_solution(7936289483170179876)
XLA Ops:
  1.3 11.2 %halo.1 = (f32[2,4,448,128]{3,2,1,0:T(8,128)S(1)}, bf16[512,512]{1,0:T(8,128)(2,1)S(1)}, bf16[512,512]{1,0:T(8,128)(2,1)S(1)}, f32[2,256,256]{2,1,0:T(8,128)S(1)...) custom-call(f32[2,192,512]{2,1,0:T(8,128)} %obj.1, f32[256,512]{1,0:T(8,128)} %constant.2.clone.table, ...), custom_call_target="tpu_custom_call" | custom-call | tf_op jit(solution)/shard_map/halo/pallas_call | solution.py:450
  12.4 0.7 %slots.1 = (f32[2,4,448,128]{3,2,1,0:T(8,128)S(1)}, f32[2,256,256]{2,1,0:T(8,128)S(1)}) custom-call(s32[1]{0:T(128)S(6)} %copy.9.cnt, s32[12]{0:T(128)S(1)} %get-tuple-element.13.row, s32[12]{0:T(128)S(1)} %get-tuple-element.14.col, f32[2,4,448,128]{3,2,1,0:T(8,128)S(1)} %get-tuple-element.15.win, f32[2,256,256]{2,1,0:T(8,128)S(1)} %get-tuple-element.16.probe, ...), custom_call_target="tpu_custom_call" | custom-call | tf_op jit(solution)/shard_map/slots/pallas_call | solution.py:479
  13.2 38.2 %merge.1 = (s16[8,208,128]{2,1,0:T(8,128)(2,1)S(1)}, f32[2,256,256]{2,1,0:T(8,128)S(1)}) custom-call(s32[1]{0:T(128)S(6)} %copy.9.cnt, s32[12]{0:T(128)S(1)} %get-tuple-element.13.row, s32[12]{0:T(128)S(1)} %get-tuple-element.14.col, f32[2,4,448,128]{3,2,1,0:T(8,128)S(1)} %get-tuple-element.15.win, f32[2,256,256]{2,1,0:T(8,128)S(1)} %get-tuple-element.16.probe, ...), custom_call_target="tpu_custom_call" | custom-call | tf_op jit(solution)/shard_map/merge/pallas_call | solution.py:496
  51.3 1.1 %finish.1 = (f32[2,192,512]{2,1,0:T(8,128)}, f32[2,256,256]{2,1,0:T(8,128)}) custom-call(s16[8,208,128]{2,1,0:T(8,128)(2,1)S(1)} %get-tuple-element.22.all_q, f32[2,256,256]{2,1,0:T(8,128)S(1)} %get-tuple-element.23.psum), custom_call_target="tpu_custom_call" | custom-call | tf_op jit(solution)/shard_map/finish/pallas_call | solution.py:521

commit v8 on v7

--- a/solution.py
+++ b/solution.py
@@ -256,8 +256,8 @@
 
 
 def merge_kernel(
-    cnt, row, col, win, probe, meas, left, right, grad, psum_in, all_q, pout,
-    spots, psum, to_core_buf, from_core, merged, qa, qb, ra, rb, qs, rs, total, other,
+    cnt, row, col, win, probe, meas, left, right, grad, psum_in, full_q, early_q, late_q, pout,
+    spots, psum, to_core_buf, from_core, merged, qa, qb, ra, rb, qs, rs, total, full, early, late,
     pcore, psumc, pxy, pz,
     core_s, core_r, a_s, a_r, b_s, b_r, sh_s, sh_r, ag_s, ag_r, pc_s, pc_r, xy_s, xy_r, z_s, z_r,
 ):
@@ -313,25 +313,34 @@
 
     pl.semaphore_wait(barrier, NX + NX * NY - 1 + NZ - 1 + jnp.minimum(CHIPS - 1 - chip, 1))
 
-    first = remote(psum.at[1 - core], pcore, pc_s.at[0], pc_r.at[0], sib)
-    first.start()
+    quarters = (2, 1, 3, 0)
+
+    def quarter(dy):
+        return pl.ds(W // NY * lax.rem(y + dy + NY, NY), W // NY)
+
+    first = [
+        remote(psum.at[1 - core, quarter(dy)], pcore.at[quarter(dy)], pc_s.at[dy], pc_r.at[dy], sib) for dy in range(NY)
+    ]
+    for dy in quarters:
+        first[dy].start()
     piece = [lax.rem(p + dx, NX) for dx in range(NX)]
     order = (2, 1, 3, 0)
     to_core = {
         dx: remote(to_core_buf.at[dx], from_core.at[dx], core_s.at[dx], core_r.at[dx], sib) for dx in order
     }
+    xy_send = {}
+    for dy in quarters:
+        first[dy].wait_recv()
+        psumc[quarter(dy), :] = psum[core, quarter(dy), :] + pcore[quarter(dy), :]
+        for i, d in enumerate(xys):
+            if d[1] == dy:
+                rows = pl.ds(16 * (NX * lax.rem(y + dy, NY) + lax.rem(p + d[0], NX)), 16)
+                xy_send[d] = remote(psumc.at[rows], pxy.at[i], xy_s.at[NY], xy_r.at[NY], at(*d))
+                xy_send[d].start()
+
     for dx in order:
         to_core_buf[dx] = window(piece[dx] // 2, 2 * (1 - core) + lax.rem(piece[dx], 2))
         to_core[dx].start()
-
-    first.wait_recv()
-    psumc[...] = psum[core] + pcore[...]
-    xy_send = []
-    for i, (dx, dy) in enumerate(xys):
-        rows = pl.ds(16 * (NX * lax.rem(y + dy, NY) + lax.rem(p + dx, NX)), 16)
-        xy_send.append(remote(psumc.at[rows], pxy.at[i], xy_s.at[0], xy_r.at[0], at(dx, dy)))
-    for copy in xy_send:
-        copy.start()
 
     a_send = {dx: remote(qa.at[dx], ra.at[dx], a_s.at[0], a_r.at[0], at(dx)) for dx in (2, 1, 3)}
     b_send = {dx: remote(qb.at[dx], rb.at[dx], b_s.at[0], b_r.at[0], at(dx)) for dx in (2, 1, 3)}
@@ -349,7 +358,7 @@
         a_send[dx].start()
 
     mine = pl.ds(16 * (NX * y + p), 16)
-    xy_all = remote(pxy, pxy, xy_s.at[0], xy_r.at[0], sib)
+    xy_all = remote(pxy, pxy, xy_s.at[NY], xy_r.at[NY], sib)
     xy_all.wait_recv()
     part = psumc[mine, :]
     for i in range(len(xys)):
@@ -359,7 +368,7 @@
     for copy in z_send:
         copy.start()
 
-    for copy in [first, xy_all] + list(to_core.values()):
+    for copy in first + [xy_all] + list(to_core.values()):
         copy.wait_send()
     others = pl.ds(1, NX - 1)
     a_all = remote(ra.at[others], ra.at[others], a_s.at[0], a_r.at[0], sib)
@@ -375,12 +384,44 @@
     a_all.wait_recv()
     total[...] = merged[0, :OWN, :] + (decode(ra.at[1], OWN) + decode(ra.at[3], OWN) + decode(ra.at[2], OWN))
 
+    slot = NX * core + p
+    even_band, odd_band = {"band": 2 * chip}, {"band": 2 * chip + 1}
+
+    def spread(src, dst, lead, k, here):
+        copies = [remote(src, dst.at[slot], ag_s.at[k], ag_r.at[k], at(dx, **lead)) for dx in order]
+        for copy in copies[:-1]:
+            copy.start()
+
+        @pl.when(core != here)
+        def _():
+            copies[-1].start()
+
+        @pl.when(core == here)
+        def _():
+            dst[slot] = src[...]
+
+    def settle(src, dst, k, here):
+        @pl.when(core == here)
+        def _():
+            seven = dst.at[pl.ds(0, 2 * NX - 1)]
+            remote(seven, seven, ag_s.at[k], ag_r.at[k], sib).wait_recv()
+
+        for count, mine_ in ((NX, 1 - here), (NX - 1, here)):
+
+            @pl.when(core == mine_)
+            def _():
+                some = dst.at[pl.ds(0, count)]
+                remote(some, some, ag_s.at[k], ag_r.at[k], sib).wait_send()
+
+    code(total[BELOW:, :], early, OWN - BELOW)
+    spread(early, early_q, odd_band, 0, 1)
+
     z_all = remote(pz.at[pl.ds(0, NZ - 1)], pz.at[pl.ds(0, NZ - 1)], z_s.at[0], z_r.at[0], sib)
     z_all.wait_recv()
     part = ((pz[0] + pz[1]) + (pz[2] + pz[3])) + ((pz[4] + pz[5]) + (pz[6] + pz[7]))
     pout[core, mine, :] = part * F32(1.0 / math.sqrt(LIVE))
     xy_back = [
-        remote(pout.at[core, mine], pout.at[core, mine], xy_s.at[1], xy_r.at[1], at(dx, dy))
+        remote(pout.at[core, mine], pout.at[core, mine], xy_s.at[dy], xy_r.at[dy], at(dx, dy))
         for i, (dx, dy) in enumerate(xys)
     ]
     for copy in xy_back:
@@ -391,16 +432,10 @@
         shift.wait_recv()
         total[:BELOW, :] += decode(rs, BELOW)
 
-    slot = NX * core + p
-    code(total[pl.ds(BR * (1 - core), BR), :], other, BR)
-    code(total[pl.ds(BR * core, BR), :], all_q.at[slot], BR)
-    gather = []
-    for dx in order:
-        gather.append(remote(other, all_q.at[slot], ag_s.at[0], ag_r.at[0], at(dx, band=sb)))
-        if dx:
-            gather.append(remote(all_q.at[slot], all_q.at[slot], ag_s.at[0], ag_r.at[0], at(dx)))
-    for copy in gather:
-        copy.start()
+    code(total[:BR, :], full, BR)
+    spread(full, full_q, even_band, 1, 0)
+    code(total[BR:BELOW, :], late, TAIL)
+    spread(late, late_q, odd_band, 2, 1)
 
     for copy in (z_all, a_all, b_all):
         copy.wait_send()
@@ -409,18 +444,26 @@
     def _():
         shift.wait_send()
 
-    back_all = remote(pxy, pxy, xy_s.at[1], xy_r.at[1], sib)
-    back_all.wait_recv()
-    last = remote(pout.at[core], pout.at[core], pc_s.at[1], pc_r.at[1], sib)
-    last.start()
-    gather_all = remote(all_q.at[pl.ds(0, 2 * NX - 1)], all_q.at[pl.ds(0, 2 * NX - 1)], ag_s.at[0], ag_r.at[0], sib)
-    gather_all.wait_recv()
-    for copy in (gather_all, back_all):
+    back = []
+    last = []
+    for dy in (0, 1, 3, 2):
+        some = pxy.at[pl.ds(0, NX if dy else NX - 1)]
+        back.append(remote(some, some, xy_s.at[dy], xy_r.at[dy], sib))
+        back[-1].wait_recv()
+        rows = quarter(-dy)
+        last.append(remote(pout.at[core, rows], pout.at[core, rows], pc_s.at[NY + dy], pc_r.at[NY + dy], sib))
+        last[-1].start()
+    settle(early, early_q, 0, 1)
+    settle(full, full_q, 1, 0)
+    settle(late, late_q, 2, 1)
+    for copy in back:
         copy.wait_send()
-    last.wait()
-
-
-def finish_kernel(all_q, psum, out, pout, buf, sems):
+    for copy in last:
+        copy.wait()
+
+
+def finish_kernel(full_q, early_q, late_q, psum, out, pout, buf, sems):
+    core = lax.rem(lax.axis_index("band"), 2)
     probe_copy = pltpu.make_async_copy(psum, pout, sems.at[2])
     probe_copy.start()
     copies = []
@@ -429,7 +472,17 @@
             for j in range(2):
                 block = 2 * c + j
                 cols = slice(block * LANES, (block + 1) * LANES)
-                buf[plane, :, cols] = decode(all_q.at[NX * c + 2 * plane + j], BR)
+                k = NX * c + 2 * plane + j
+
+                @pl.when(core == 0)
+                def _():
+                    buf[plane, :, cols] = decode(full_q.at[k], BR)
+
+                @pl.when(core == 1)
+                def _():
+                    buf[plane, :TAIL, cols] = decode(late_q.at[k], TAIL)
+                    buf[plane, TAIL:, cols] = decode(early_q.at[k], BR - TAIL)
+
         copies.append(pltpu.make_async_copy(buf.at[plane], out.at[plane], sems.at[plane]))
         copies[plane].start()
     for copy in copies + [probe_copy]:
@@ -497,39 +550,43 @@
         merge_kernel,
         out_shape=(
             jax.ShapeDtypeStruct((2 * NX, BR + EXTRA, LANES), jnp.int16),
+            jax.ShapeDtypeStruct((2 * NX, BR - TAIL + EXTRA, LANES), jnp.int16),
+            jax.ShapeDtypeStruct((2 * NX, TAIL + EXTRA, LANES), jnp.int16),
             jax.ShapeDtypeStruct((2, W, W), F32),
         ),
         in_specs=[SM] * 3 + [VM] * 7,
-        out_specs=(VM, VM),
+        out_specs=(VM, VM, VM, VM),
         scratch_shapes=[
             piece(W + 2 * BR, GROUP, 2, BLOCKS), flat(W, 2),
             piece(ROWS, NX), piece(ROWS, NX), piece(CHIP, NX),
             coded(OWN, NX), coded(BELOW, NX), coded(OWN, NX), coded(BELOW, NX), coded(BELOW), coded(BELOW),
-            piece(OWN), coded(BR),
+            piece(OWN), coded(BR), coded(BR - TAIL), coded(TAIL),
             flat(W), flat(W), flat(16, 15), flat(16, NZ),
         ]
         + [DMA((NX,))] * 2
-        + [DMA((1,))] * 8
-        + [DMA((2,))] * 4
+        + [DMA((1,))] * 6
+        + [DMA((3,))] * 2
+        + [DMA((2 * NY,))] * 2
+        + [DMA((NY + 1,))] * 2
         + [DMA((1,))] * 2,
         compiler_params=params(1),
         name="merge",
     )(counts, rows, cols, win, probe, measured, left, right, grad, psum)
 
 
-def finish(all_q, psum):
+def finish(full_q, early_q, late_q, psum):
     return pl.pallas_call(
         finish_kernel,
         out_shape=(
             jax.ShapeDtypeStruct((2, BR, NCOLS), F32),
             jax.ShapeDtypeStruct((2, W, W), F32),
         ),
-        in_specs=[VM, VM],
+        in_specs=[VM] * 4,
         out_specs=(HBM, HBM),
         scratch_shapes=[pltpu.VMEM((2, BR, NCOLS), F32), DMA((3,))],
         compiler_params=params(),
         name="finish",
-    )(all_q, psum)
+    )(full_q, early_q, late_q, psum)
 
 
 def on_device(object_field, probe, measured, row_offset, col_offset, counts):

time: 52.4 us -> 53.2 us (1.015)
  Pallas kernels: 51.1 us -> 52 us
    pallas_call x1, Pallas kernels: 38.2 us -> 39.1 us  [merge(): pl.pallas_call(merge_kernel, out_shape=(jax.ShapeDtypeStruct((2 * NX, BR...]
where the time goes in v8:
time: 53.2 us; the launch traced here: 53.5 us
  Pallas kernels  52 us (98%)
  between operations  1.46 us (3%)
    pallas_call x1, Pallas kernels, merge(): pl.pallas_call(merge_kernel, out_shape=(jax.ShapeDtypeStruct((2 * NX, BR...  39.1 us
    pallas_call x1, Pallas kernels, halo(): pl.pallas_call(halo_kernel, out_shape=(jax.ShapeDtypeStruct((2, BLOCKS, R...  11.2 us
    pallas_call x1, Pallas kernels, finish(): pl.pallas_call(finish_kernel, out_shape=(jax.ShapeDtypeStruct((2, BR, NCO...  1.08 us

profile of v8, /device:TPU:1, one launch (start us, length us, event | category | flops | bytes accessed | tf_op | source)
XLA Modules:
  0.0 53.5 jit_solution(12909926571992334063)
XLA Ops:
  1.3 11.2 %halo.1 = (f32[2,4,448,128]{3,2,1,0:T(8,128)S(1)}, bf16[512,512]{1,0:T(8,128)(2,1)S(1)}, bf16[512,512]{1,0:T(8,128)(2,1)S(1)}, f32[2,256,256]{2,1,0:T(8,128)S(1)...) custom-call(f32[2,192,512]{2,1,0:T(8,128)} %obj.1, f32[256,512]{1,0:T(8,128)} %constant.2.clone.table, ...), custom_call_target="tpu_custom_call" | custom-call | tf_op jit(solution)/shard_map/halo/pallas_call | solution.py:503
  12.4 0.7 %slots.1 = (f32[2,4,448,128]{3,2,1,0:T(8,128)S(1)}, f32[2,256,256]{2,1,0:T(8,128)S(1)}) custom-call(s32[1]{0:T(128)S(6)} %copy.9.cnt, s32[12]{0:T(128)S(1)} %get-tuple-element.15.row, s32[12]{0:T(128)S(1)} %get-tuple-element.16.col, f32[2,4,448,128]{3,2,1,0:T(8,128)S(1)} %get-tuple-element.17.win, f32[2,256,256]{2,1,0:T(8,128)S(1)} %get-tuple-element.18.probe, ...), custom_call_target="tpu_custom_call" | custom-call | tf_op jit(solution)/shard_map/slots/pallas_call | solution.py:532
  13.2 39.1 %merge.1 = (s16[8,208,128]{2,1,0:T(8,128)(2,1)S(1)}, s16[8,144,128]{2,1,0:T(8,128)(2,1)S(1)}, s16[8,80,128]{2,1,0:T(8,128)(2,1)S(1)}, f32[2,256,256]{2,1,0:T(8,128)S(1)}) custom-call(s32[1]{0:T(128)S(6)} %copy.9.cnt, s32[12]{0:T(128)S(1)} %get-tuple-element.15.row, s32[12]{0:T(128)S(1)} %get-tuple-element.16.col, ...), custom_call_target="tpu_custom_call" | custom-call | tf_op jit(solution)/shard_map/merge/pallas_call | solution.py:549
  52.2 1.1 %finish.1 = (f32[2,192,512]{2,1,0:T(8,128)}, f32[2,256,256]{2,1,0:T(8,128)}) custom-call(s16[8,208,128]{2,1,0:T(8,128)(2,1)S(1)} %get-tuple-element.24.full_q, s16[8,144,128]{2,1,0:T(8,128)(2,1)S(1)} %get-tuple-element.25.early_q, s16[8,80,128]{2,1,0:T(8,128)(2,1)S(1)} %get-tuple-element.26.late_q, f32[2,256,256]{2,1,0:T(8,128)S(1)} %get-tuple-element.27.psum), custom_call_target="tpu_custom_call" | custom-call | tf_op jit(solution)/shard_map/finish/pallas_call | solution.py:578
